TPU v7x, 32 devices: a whole 2x2x4 slice. The times are simulated.
32 devices in a mesh: grp: 2 (over x), sx: 16 (over z, y, core).
Axes of the slice: x: 2, y: 2, z: 4, core: 2. Of those that a mesh axis runs over, the one named last changes fastest.
Arguments:
- right_side: float32 [128, 256, 128], P(('grp', 'sx')), parts along dimension 0, may hold values from -6 to 6
- storage: float32 [128, 256, 128], P(('grp', 'sx')), parts along dimension 0, may hold values from 0.05 to 0.5
- trans_x: float32 [512, 128], P('grp'), parts along dimension 0, may hold values from 0.1 to 1
- trans_y: float32 [128, 256, 128], P(('grp', 'sx')), parts along dimension 0, may hold values from 0.1 to 1
- trans_z: float32 [128, 256, 128], P(('grp', 'sx')), parts along dimension 0, may hold values from 0.1 to 1
- well_cells: int32 [32], P('grp'), parts along dimension 0, may hold values from 0 to 2097151
- well_rates: float32 [32], P('grp'), parts along dimension 0, may hold values from -40 to 40
- sat_logit: float32 [128, 256, 128], P(('grp', 'sx')), parts along dimension 0, may hold values from -8 to 8
- porosity: float32 [128, 256, 128], P(('grp', 'sx')), parts along dimension 0, may hold values from 0.1 to 0.3
- y_index: int32 [128], replicated, may hold values from -1 to 62, as said below
- y_frac: float32 [128], replicated, may hold values from 0 to 1
- z_index: int32 [256], replicated, may hold values from -1 to 126, as said below
- z_frac: float32 [256], replicated, may hold values from 0 to 1
- background: float32 [128, 512, 256], P(None, ('grp', 'sx')), parts along dimension 1, may hold values from 0.55 to 0.85
- wave_prev: float32 [128, 512, 256], P(None, ('grp', 'sx')), parts along dimension 1, may hold values from -6 to 6
- wave_now: float32 [128, 512, 256], P(None, ('grp', 'sx')), parts along dimension 1, may hold values from -6 to 6
- data_residual: float32 [128, 512, 256], P(None, ('grp', 'sx')), parts along dimension 1, may hold values from -6 to 6
Outputs:
- pressure: float32 [128, 256, 128], P(('grp', 'sx')), parts along dimension 0
- wavefield: float32 [128, 512, 256], P(None, ('grp', 'sx')), parts along dimension 1
- sat_gradient: float32 [128, 256, 128], P(('grp', 'sx')), parts along dimension 0
There are 2 independent parts, one for each index of `grp`. A program takes and returns all parts, laid end to end along the dimension named above; an argument that names none is the same for every part. Nothing has to cross between parts.
Inputs may be any that keep to these rules, and one draw needn't show every extreme that they name: -1 marks a seismic row outside the reservoir; otherwise cells y_index and y_index + 1 along i are blended. -1 marks a depth outside the reservoir; otherwise layers z_index and z_index + 1 are blended. `well_cells`: flat index (i * 256 + j) * 128 + k; a cell may hold several wells.
All inputs are finite; a program needn't handle non-finite values.
Results may differ from a plain program's by a relative error of at most 0.0003.
Values sent between devices are 32-bit elements; how exact they have to be, the bound alone decides.
A program may use at most 128 MiB of HBM per device.

v0:
```python
import jax
import jax.numpy as jnp
from jax import lax
from jax.sharding import PartitionSpec as P

ITERS = 2
STEPS = 4


courant = 0.25
transport = 2.0
velocity_ref = 22.5
mineral_bulk = 37.0
mineral_shear = 44.0
carbon_bulk = 0.08
brine_bulk = 2.5
mineral_density = 2.65
carbon_density = 0.7
brine_density = 1.03


def extended(block, sides, width):
    for axis, dim in sides:
        count = lax.axis_size(axis)
        forward = [(i, i + 1) for i in range(count - 1)]
        backward = [(target, source) for source, target in forward]
        low = lax.ppermute(
            lax.slice_in_dim(block, block.shape[dim] - width, None, axis=dim), axis, forward
        )
        high = lax.ppermute(lax.slice_in_dim(block, 0, width, axis=dim), axis, backward)
        block = jnp.concatenate([low, block, high], axis=dim)
    return block


def lateral(values, trans_y, trans_z):
    upper_y = jnp.pad(values[:, 1:], ((0, 0), (0, 1), (0, 0)))
    lower_y = jnp.pad(values[:, :-1], ((0, 0), (1, 0), (0, 0)))
    below_y = jnp.pad(trans_y[:, :-1], ((0, 0), (1, 0), (0, 0)))
    upper_z = jnp.pad(values[:, :, 1:], ((0, 0), (0, 0), (0, 1)))
    lower_z = jnp.pad(values[:, :, :-1], ((0, 0), (0, 0), (1, 0)))
    below_z = jnp.pad(trans_z[:, :, :-1], ((0, 0), (0, 0), (1, 0)))
    return (
        trans_y * (values - upper_y)
        + below_y * (values - lower_y)
        + trans_z * (values - upper_z)
        + below_z * (values - lower_z)
    )


def flow_apply(values, storage, trans_x, trans_y, trans_z):
    padded = extended(values, (("sx", 0),), 1)
    along_i = trans_x[None] * (2.0 * values - padded[2:] - padded[:-2])
    return storage * values + along_i + lateral(values, trans_y, trans_z)


def global_sum(values):
    return lax.psum(values, "sx")


def perturb(saturation, porosity):
    fluid_bulk = 1.0 / (saturation / carbon_bulk + (1.0 - saturation) / brine_bulk)
    frame_factor = (1.0 - porosity) ** 3
    dry_bulk = mineral_bulk * frame_factor
    shear_mod = mineral_shear * frame_factor
    biot_ratio = 1.0 - dry_bulk / mineral_bulk
    sat_bulk = dry_bulk + biot_ratio * biot_ratio / (
        porosity / fluid_bulk
        + (1.0 - porosity) / mineral_bulk
        - dry_bulk / (mineral_bulk * mineral_bulk)
    )
    density = mineral_density * (1.0 - porosity) + porosity * (
        carbon_density * saturation + brine_density * (1.0 - saturation)
    )
    return (sat_bulk + 4.0 / 3.0 * shear_mod) / density / velocity_ref - 1.0


def blend_matrix(positions, fraction, extent):
    columns = jnp.arange(extent, dtype=jnp.int32)[None, :]
    lower_w = (columns == positions[:, None]).astype(jnp.float32) * (1.0 - fraction)[:, None]
    upper_hit = (columns == (positions + 1)[:, None]) & (positions[:, None] >= 0)
    return lower_w + upper_hit.astype(jnp.float32) * fraction[:, None]


def laplace_padded(padded):
    centre = padded[:, 1:-1]
    padded_yz = jnp.pad(centre, ((1, 1), (0, 0), (1, 1)))
    total = padded[:, 2:] + padded[:, :-2]
    total = total + padded_yz[2:, :, 1:-1] + padded_yz[:-2, :, 1:-1]
    total = total + padded_yz[1:-1, :, 2:] + padded_yz[1:-1, :, :-2]
    return total - 6.0 * centre


def wave_laplace(values):
    return laplace_padded(extended(values, (("sx", 1),), 1))


def run_wave(previous, current, model_field, final_cotangent, apply_laplace):
    stencils = []
    for number in range(STEPS):
        stencil = apply_laplace(current)
        stencils.append(stencil)
        following = 2.0 * current - previous + courant * model_field * stencil
        previous, current = (current, following)
    adjoint = final_cotangent
    adjoint_late = jnp.zeros_like(final_cotangent)
    gradient = jnp.zeros_like(final_cotangent)
    for number in reversed(range(STEPS)):
        gradient = gradient + courant * stencils[number] * adjoint
        if number > 0:
            earlier = 2.0 * adjoint + courant * apply_laplace(model_field * adjoint) - adjoint_late
            adjoint_late, adjoint = (adjoint, earlier)
    return (current, gradient)


def per_device(
    right_side,
    storage,
    trans_x,
    trans_y,
    trans_z,
    well_cells,
    well_rates,
    sat_logit,
    porosity,
    y_index,
    y_frac,
    z_index,
    z_frac,
    background,
    wave_prev,
    wave_now,
    data_residual,
):
    i_rows, columns, layers = right_side.shape
    cell_count = i_rows * columns * layers
    offset = lax.axis_index("sx") * cell_count
    local_cell = well_cells - offset
    inside = (local_cell >= 0) & (local_cell < cell_count)
    source = (
        jnp.zeros((cell_count,), jnp.float32)
        .at[jnp.where(inside, local_cell, 0)]
        .add(jnp.where(inside, well_rates, 0.0))
        .reshape(i_rows, columns, layers)
    )
    forcing = right_side + source
    pressure = jnp.zeros_like(forcing)
    residual = forcing
    direction = forcing
    norm_now = global_sum(jnp.sum(residual * residual))
    for number in range(ITERS):
        image = flow_apply(direction, storage, trans_x, trans_y, trans_z)
        alpha = norm_now / global_sum(jnp.sum(direction * image))
        pressure = pressure + alpha * direction
        residual = residual - alpha * image
        norm_next = global_sum(jnp.sum(residual * residual))
        direction = residual + norm_next / norm_now * direction
        norm_now = norm_next
    inflow = storage * pressure - flow_apply(pressure, storage, trans_x, trans_y, trans_z) + source
    saturation = jax.nn.sigmoid(sat_logit + transport * inflow)
    change, pull = jax.vjp(lambda sat_value: perturb(sat_value, porosity), saturation)
    received = lax.all_to_all(change, "sx", split_axis=1, concat_axis=0, tiled=True)
    i_cells, planes, depth_cells = received.shape
    weight_y = blend_matrix(y_index, y_frac, i_cells)
    weight_z = blend_matrix(z_index, z_frac, depth_cells)
    seis_y = weight_y.shape[0]
    seis_z = weight_z.shape[0]
    depth = jnp.dot(
        received.reshape(i_cells * planes, depth_cells), weight_z.T, precision=lax.Precision.HIGHEST
    )
    lifted = jnp.dot(
        weight_y, depth.reshape(i_cells, planes * seis_z), precision=lax.Precision.HIGHEST
    )
    model = background + lifted.reshape(seis_y, planes, seis_z)
    wavefield, gradient = run_wave(wave_prev, wave_now, model, data_residual, wave_laplace)
    spread = jnp.dot(
        weight_y.T, gradient.reshape(seis_y, planes * seis_z), precision=lax.Precision.HIGHEST
    )
    restricted = jnp.dot(
        spread.reshape(i_cells * planes, seis_z), weight_z, precision=lax.Precision.HIGHEST
    )
    returned = lax.all_to_all(
        restricted.reshape(i_cells, planes, depth_cells),
        "sx",
        split_axis=0,
        concat_axis=1,
        tiled=True,
    )
    (sat_gradient,) = pull(returned)
    return (pressure, wavefield, sat_gradient)


def solution(mesh):
    in_specs = (
        P(("grp", "sx"), None, None),
        P(("grp", "sx"), None, None),
        P("grp", None),
        P(("grp", "sx"), None, None),
        P(("grp", "sx"), None, None),
        P("grp"),
        P("grp"),
        P(("grp", "sx"), None, None),
        P(("grp", "sx"), None, None),
        P(),
        P(),
        P(),
        P(),
        P(None, ("grp", "sx"), None),
        P(None, ("grp", "sx"), None),
        P(None, ("grp", "sx"), None),
        P(None, ("grp", "sx"), None),
    )
    out_specs = (
        P(("grp", "sx"), None, None),
        P(None, ("grp", "sx"), None),
        P(("grp", "sx"), None, None),
    )
    return jax.shard_map(
        per_device, mesh=mesh, in_specs=in_specs, out_specs=out_specs, check_vma=False
    )
```

profile of v0, /device:TPU:0, one launch (start us, length us, event | category | flops | bytes accessed | tf_op | source)
XLA Modules:
  0.0 323.2 jit_solution(7126526452341134337)
XLA Ops:
  0.6 0.8 compare_select_fusion
  1.5 0.7 broadcast_select_fusion
  2.1 0.8 scatter_custom_fusion
  3.0 1.3 add.294
  4.3 1.3 collective-permute-start
  5.6 3.0 collective-permute-start.1
  8.6 1.2 copy.115
  9.9 0.8 fusion.147
  10.6 1.3 collective-permute-start.6
  12.0 5.9 %collective-permute-start.7 = (f32[128,1,256]{2,0,1:T(8,128)}, f32[128,1,256]{2,0,1:T(8,128)}, u32[]{:S(2)}, u32[]{:S(2)}) collective-permute-start(f32[128,1,256]{2,0,1:T(8,128)} %get-tuple-element.51), channel_id=1, source_target_pairs={{0,1},{1,2},{2,3},{3,4},{4,5},{5,6},{6,7},{7,8},{8,9},{9,10},{10,1... | collective-permute-start | bytes 393224 | tf_op jit(solution)/shard_map/ppermute | solution.py:27
  18.0 0.2 fusion.158
  18.2 2.1 multiply_reduce_fusion.1
  20.4 33.0 %all-reduce.21 = (f32[]{:T(128)}, f32[]{:T(128)}) all-reduce(f32[]{:T(128)} %get-tuple-element.19, f32[]{:T(128)} %get-tuple-element.18), channel_id=1, replica_groups=mesh['grp'=2,'sx'=16] {'sx'}, use_global_device_ids=true, to_apply=%region_2.3 | all-reduce | flops 2 | bytes 16 | tf_op jit(solution)/shard_map/psum | solution.py:57
  54.5 3.1 multiply_reduce_fusion
  57.7 30.1 %psum.30 = f32[]{:T(128)} all-reduce(f32[]{:T(128)} %get-tuple-element.36), channel_id=1, replica_groups=mesh['grp'=2,'sx'=16] {'sx'}, use_global_device_ids=true, to_apply=%region_6.7 | all-reduce | flops 1 | bytes 8 | tf_op jit(solution)/shard_map/psum | solution.py:57
  89.0 1.1 multiply_add_fusion.9
  90.2 0.2 fusion.155
  90.4 1.4 collective-permute-start.2
  91.8 3.0 collective-permute-start.3
  95.0 0.9 collective-permute-done.3
  95.8 1.2 fusion.77
  97.1 32.0 %psum.31 = f32[]{:T(128)} all-reduce(f32[]{:T(128)} %fusion.77), channel_id=1, replica_groups=mesh['grp'=2,'sx'=16] {'sx'}, use_global_device_ids=true, to_apply=%region_8.9 | all-reduce | flops 1 | bytes 8 | tf_op jit(solution)/shard_map/psum | solution.py:57
  130.4 1.1 multiply_add_fusion.8
  131.6 0.2 fusion.153
  131.8 1.4 collective-permute-start.4
  133.2 3.0 collective-permute-start.5
  136.4 0.9 collective-permute-done.5
  137.3 1.9 multiply_add_fusion.4
  139.2 1.1 copy.117
  140.4 4.7 %all-to-all-start = ((f32[4,256,128]{2,0,1:T(4,128)}), f32[4,256,128]{2,0,1:T(4,128)S(1)}, u32[]{:S(2)}, u32[]{:S(2)}) async-start(f32[4,256,128]{2,0,1:T(4,128)} %copy.117), calls=%async_computation | async-start | bytes 1048576 | tf_op jit(solution)/shard_map/all_to_all | solution.py:161
  145.2 14.4 %all-to-all-done = f32[4,256,128]{2,0,1:T(4,128)S(1)} async-done(((f32[4,256,128]{2,0,1:T(4,128)}), f32[4,256,128]{2,0,1:T(4,128)S(1)}, u32[]{:S(2)}, u32[]{:S(2)}) %all-to-all-start) | async-done | bytes 524320 | tf_op jit(solution)/shard_map/all_to_all | solution.py:161
  159.6 2.2 fusion.98
  161.8 1.4 reshape.45
  163.2 15.2 %fusion.54 = (f32[128,16,256]{2,0,1:T(8,128)S(1)}, f32[128,16,256]{2,0,1:T(8,128)}, f32[128,16,256]{2,0,1:T(8,128)S(1)}, f32[128,16,256]{2,0,1:T(8,128)}) fusion(f32[128,16,256]{2,1,0:T(8,128)} %param.31, f32[128,16,256]{2,1,0:T(8,128)S(1)} %copy-done, f32[128,16,256]{2,0,1:T(8,128)} %copy-done.8, f32[128,1,256]{2,0,1:T(8,128)} %collective-permute-done.7, ...), kind=kOutput, calls=%fused_computation.99 | convolution fusion | flops 411090944 | bytes 20187264 | tf_op jit(solution)/shard_map/dot_general | solution.py:170
  178.5 1.3 copy-done.6
  179.8 1.3 collective-permute-start.8
  181.1 3.0 collective-permute-start.9
  184.2 1.3 collective-permute-start.14
  185.5 3.8 %collective-permute-start.15 = (f32[128,1,256]{2,0,1:T(8,128)S(1)}, f32[128,1,256]{2,0,1:T(8,128)S(1)}, u32[]{:S(2)}, u32[]{:S(2)}) collective-permute-start(f32[128,1,256]{2,0,1:T(8,128)S(1)} %get-tuple-element.57), channel_id=1, source_target_pairs={{0,1},{1,2},{2,3},{3,4},{4,5},{5,6},{6,7},{7,8},{8,9},{9,10},{10,1... | collective-permute-start | bytes 393224 | tf_op jit(solution)/shard_map/ppermute | solution.py:27
  189.3 0.9 collective-permute-done.15
  190.3 23.2 %multiply_add_fusion.2 = (f32[128,16,256]{2,0,1:T(8,128)}, f32[128,16,256]{2,0,1:T(8,128)}, f32[128,16,256]{2,0,1:T(8,128)}, f32[128,16,256]{2,0,1:T(8,128)}) fusion(f32[128,16,256]{2,0,1:T(8,128)} %get-tuple-element.76, f32[128,16,256]{2,0,1:T(8,128)} %get-tuple-element.33, f32[128,16,256]{2,1,0:T(8,128)} %param.31, f32[128,16,256]{2,1,0:T(8,128)S(1)} %copy-done, ...), kind=kLoop, calls=%fused_computation.102 | loop fusion | flops 16252928 | bytes 23592960 | tf_op jit(solution)/shard_map/add | solution.py:102
  213.5 1.0 fusion.145
  214.5 1.3 collective-permute-start.10
  215.8 6.2 %collective-permute-start.11 = (f32[128,1,256]{2,0,1:T(8,128)S(1)}, f32[128,1,256]{2,0,1:T(8,128)S(1)}, u32[]{:S(2)}, u32[]{:S(2)}) collective-permute-start(f32[128,1,256]{2,0,1:T(8,128)S(1)} %get-tuple-element.44), channel_id=1, source_target_pairs={{0,1},{1,2},{2,3},{3,4},{4,5},{5,6},{6,7},{7,8},{8,9},{9,10},{10,1... | collective-permute-start | bytes 393224 | tf_op jit(solution)/shard_map/ppermute | solution.py:27
  221.9 1.0 fusion.149
  222.9 1.3 collective-permute-start.16
  224.2 5.0 %collective-permute-start.17 = (f32[128,1,256]{2,0,1:T(8,128)S(1)}, f32[128,1,256]{2,0,1:T(8,128)S(1)}, u32[]{:S(2)}, u32[]{:S(2)}) collective-permute-start(f32[128,1,256]{2,0,1:T(8,128)S(1)} %get-tuple-element.55), channel_id=1, source_target_pairs={{0,1},{1,2},{2,3},{3,4},{4,5},{5,6},{6,7},{7,8},{8,9},{9,10},{10,1... | collective-permute-start | bytes 393224 | tf_op jit(solution)/shard_map/ppermute | solution.py:27
  229.3 0.9 collective-permute-done.17
  230.2 18.7 %multiply_add_fusion.1 = (f32[128,16,256]{2,0,1:T(8,128)S(1)}, f32[128,16,256]{2,0,1:T(8,128)}, f32[128,16,256]{2,0,1:T(8,128)S(1)}, f32[128,16,256]{2,0,1:T(8,128)}) fusion(f32[128,16,256]{2,0,1:T(8,128)} %get-tuple-element.76, f32[128,16,256]{2,0,1:T(8,128)} %get-tuple-element.31, f32[128,16,256]{2,0,1:T(8,128)} %get-tuple-element.33, ...), kind=kLoop, calls=%fused_computation.101 | loop fusion | flops 18874368 | bytes 27787264 | tf_op jit(solution)/shard_map/add | solution.py:102
  248.9 1.3 copy-done.9
  250.2 1.3 collective-permute-start.12
  251.5 6.6 %collective-permute-start.13 = (f32[128,1,256]{2,0,1:T(8,128)S(1)}, f32[128,1,256]{2,0,1:T(8,128)S(1)}, u32[]{:S(2)}, u32[]{:S(2)}) collective-permute-start(f32[128,1,256]{2,0,1:T(8,128)S(1)} %get-tuple-element.40), channel_id=1, source_target_pairs={{0,1},{1,2},{2,3},{3,4},{4,5},{5,6},{6,7},{7,8},{8,9},{9,10},{10,1... | collective-permute-start | bytes 393224 | tf_op jit(solution)/shard_map/ppermute | solution.py:27
  258.2 1.3 collective-permute-start.18
  259.5 5.2 %collective-permute-start.19 = (f32[128,1,256]{2,0,1:T(8,128)S(1)}, f32[128,1,256]{2,0,1:T(8,128)S(1)}, u32[]{:S(2)}, u32[]{:S(2)}) collective-permute-start(f32[128,1,256]{2,0,1:T(8,128)S(1)} %get-tuple-element.53), channel_id=1, source_target_pairs={{0,1},{1,2},{2,3},{3,4},{4,5},{5,6},{6,7},{7,8},{8,9},{9,10},{10,1... | collective-permute-start | bytes 393224 | tf_op jit(solution)/shard_map/ppermute | solution.py:27
  264.8 0.7 collective-permute-done.19
  265.5 21.2 %fusion.44 = (f32[128,16,256]{2,0,1:T(8,128)}, f32[128,16,256]{2,0,1:T(8,128)}) fusion(f32[128,16,256]{2,0,1:T(8,128)} %get-tuple-element.46, f32[128,16,256]{2,0,1:T(8,128)} %copy-done.10, f32[128,1,256]{2,0,1:T(8,128)S(1)} %collective-permute-done.19, f32[128,1,256]{2,0,1:T(8,128)S(1)} %collective-permute-done.18, f32[128,16,256]{2,0,1:T(8,128)} %get-tuple-element.42, ...), kind=kLoop, calls=%fused_computation.73 | loop fusion | flops 17301504 | bytes 21495808 | tf_op jit(solution)/shard_map/add | solution.py:108
  286.6 2.9 copy.133
  289.5 4.0 %fusion.52 = f32[64,16,256]{2,0,1:T(8,128)S(1)} fusion(f32[128,16,256]{0,2,1:T(8,128)} %copy.133, f32[128]{0:T(128)S(1)} %copy-done.24, s32[128]{0:T(128)S(1)} %broadcast_add_fusion.1, f32[128]{0:T(128)S(1)} %broadcast_subtract_fusion.1, s32[128]{0:T(128)S(1)} %copy-done.25, pred[128]{0:T(512)(128)(4,1)S(1)} %broadcast_compare_fusion.1), kind=kOutput, calls=%fused_computation.95 | convolution fusion | flops 402702336 | bytes 3147904 | tf_op jit(solution)/shard_map/dot_general | solution.py:175
  293.5 2.4 fusion.57
  295.9 10.9 %all-to-all-start.1 = ((f32[64,16,128]{2,1,0:T(8,128)}), f32[64,16,128]{2,1,0:T(8,128)S(1)}, u32[]{:S(2)}, u32[]{:S(2)}) async-start(f32[64,16,128]{2,1,0:T(8,128)} %fusion.57), calls=%async_computation.1 | async-start | bytes 1048576 | tf_op jit(solution)/shard_map/all_to_all | solution.py:181
  306.9 7.9 %multiply_add_fusion = f32[128,16,256]{2,0,1:T(8,128)S(1)} fusion(f32[128,16,256]{2,0,1:T(8,128)} %get-tuple-element.23, f32[128,16,256]{2,0,1:T(8,128)} %get-tuple-element.76, f32[128,16,256]{2,0,1:T(8,128)} %get-tuple-element.29, f32[128,16,256]{2,0,1:T(8,128)} %get-tuple-element.31, f32[128,16,256]{2,0,1:T(8,128)} %get-tuple-element.33, ...), kind=kLoop, calls=%fused_computation.100 | loop fusion | flops 8912896 | bytes 16777216 | tf_op jit(solution)/shard_map/add | solution.py:102
  314.8 2.5 copy.136
  317.3 4.0 %all-to-all-done.1 = f32[64,16,128]{2,1,0:T(8,128)S(1)} async-done(((f32[64,16,128]{2,1,0:T(8,128)}), f32[64,16,128]{2,1,0:T(8,128)S(1)}, u32[]{:S(2)}, u32[]{:S(2)}) %all-to-all-start.1) | async-done | bytes 524320 | tf_op jit(solution)/shard_map/all_to_all | solution.py:181
  321.5 1.8 multiply_add_fusion.3
  (85 shorter events, 0.7 us)
Async XLA Ops:
  0.6 8.0 %copy-start = (f32[128,16,256]{2,1,0:T(8,128)S(1)}, f32[128,16,256]{2,1,0:T(8,128)}, u32[]{:S(2)}) copy-start(f32[128,16,256]{2,1,0:T(8,128)} %param.32) | copy-start | bytes 6291460
  3.0 6.9 %copy-start.14 = (f32[131072]{0:T(1024)}, f32[131072]{0:T(1024)S(1)}, u32[]{:S(2)}) copy-start(f32[131072]{0:T(1024)S(1)} %scatter_custom_fusion) | copy-start | bytes 1572868
  4.3 13.9 %collective-permute-start = (f32[1,256,128]{2,1,0:T(8,128)S(1)}, f32[1,256,128]{2,1,0:T(8,128)S(1)}, u32[]{:S(2)}, u32[]{:S(2)}) collective-permute-start(f32[1,256,128]{2,1,0:T(8,128)S(1)} %get-tuple-element.74), channel_id=1, source_target_pairs={{1,0},{2,1},{3,2},{4,3},{5,4},{6,5},{7,6},{8,7},{9,8},{10,9},{11,1... | collective-permute-start | bytes 393224 | tf_op jit(solution)/shard_map/ppermute | solution.py:30
  5.6 12.6 %collective-permute-start.1 = (f32[1,256,128]{2,1,0:T(8,128)S(1)}, f32[1,256,128]{2,1,0:T(8,128)S(1)}, u32[]{:S(2)}, u32[]{:S(2)}) collective-permute-start(f32[1,256,128]{2,1,0:T(8,128)S(1)} %get-tuple-element.75), channel_id=1, source_target_pairs={{0,1},{1,2},{2,3},{3,4},{4,5},{5,6},{6,7},{7,8},{8,9},{9,10},{10,1... | collective-permute-start | bytes 393224 | tf_op jit(solution)/shard_map/ppermute | solution.py:27
  9.9 8.3 %copy-start.8 = (f32[128,16,256]{2,0,1:T(8,128)}, f32[128,16,256]{2,0,1:T(8,128)S(1)}, u32[]{:S(2)}) copy-start(f32[128,16,256]{2,0,1:T(8,128)S(1)} %copy.115) | copy-start | bytes 6291460
  10.6 152.6 %collective-permute-start.6 = (f32[128,1,256]{2,0,1:T(8,128)}, f32[128,1,256]{2,0,1:T(8,128)}, u32[]{:S(2)}, u32[]{:S(2)}) collective-permute-start(f32[128,1,256]{2,0,1:T(8,128)} %get-tuple-element.50), channel_id=1, source_target_pairs={{1,0},{2,1},{3,2},{4,3},{5,4},{6,5},{7,6},{8,7},{9,8},{10,9},{11,1... | collective-permute-start | bytes 393224 | tf_op jit(solution)/shard_map/ppermute | solution.py:30
  11.9 6.3 %copy-start.1 = (f32[4,256,128]{2,1,0:T(8,128)S(1)}, f32[4,256,128]{2,1,0:T(8,128)}, u32[]{:S(2)}) copy-start(f32[4,256,128]{2,1,0:T(8,128)} %param.21) | copy-start | bytes 1572868
  11.9 6.3 %copy-start.3 = (f32[4,256,128]{2,1,0:T(8,128)S(1)}, f32[4,256,128]{2,1,0:T(8,128)}, u32[]{:S(2)}) copy-start(f32[4,256,128]{2,1,0:T(8,128)} %param.20) | copy-start | bytes 1572868
  12.0 6.3 %copy-start.11 = (f32[4,256,128]{2,1,0:T(8,128)S(1)}, f32[4,256,128]{2,1,0:T(8,128)}, u32[]{:S(2)}) copy-start(f32[4,256,128]{2,1,0:T(8,128)} %param.18) | copy-start | bytes 1572868
  12.0 6.3 %copy-start.17 = (f32[256,128]{1,0:T(8,128)S(1)}, f32[256,128]{1,0:T(8,128)}, u32[]{:S(2)}) copy-start(f32[256,128]{1,0:T(8,128)} %param.19) | copy-start | bytes 393220
  12.0 151.3 %collective-permute-start.7 = (f32[128,1,256]{2,0,1:T(8,128)}, f32[128,1,256]{2,0,1:T(8,128)}, u32[]{:S(2)}, u32[]{:S(2)}) collective-permute-start(f32[128,1,256]{2,0,1:T(8,128)} %get-tuple-element.51), channel_id=1, source_target_pairs={{0,1},{1,2},{2,3},{3,4},{4,5},{5,6},{6,7},{7,8},{8,9},{9,10},{10,1... | collective-permute-start | bytes 393224 | tf_op jit(solution)/shard_map/ppermute | solution.py:27
  18.2 2.2 copy-start.16
  90.2 5.7 %copy-start.4 = (f32[4,256,128]{2,1,0:T(8,128)S(1)}, f32[4,256,128]{2,1,0:T(8,128)}, u32[]{:S(2)}) copy-start(f32[4,256,128]{2,1,0:T(8,128)} %param.20) | copy-start | bytes 1572868
  90.2 5.7 %copy-start.12 = (f32[4,256,128]{2,1,0:T(8,128)S(1)}, f32[4,256,128]{2,1,0:T(8,128)}, u32[]{:S(2)}) copy-start(f32[4,256,128]{2,1,0:T(8,128)} %param.18) | copy-start | bytes 1572868
  90.4 4.6 %collective-permute-start.2 = (f32[1,256,128]{2,1,0:T(8,128)S(1)}, f32[1,256,128]{2,1,0:T(8,128)S(1)}, u32[]{:S(2)}, u32[]{:S(2)}) collective-permute-start(f32[1,256,128]{2,1,0:T(8,128)S(1)} %get-tuple-element.68), channel_id=1, source_target_pairs={{1,0},{2,1},{3,2},{4,3},{5,4},{6,5},{7,6},{8,7},{9,8},{10,9},{11,1... | collective-permute-start | bytes 393224 | tf_op jit(solution)/shard_map/ppermute | solution.py:30
  91.8 4.0 %collective-permute-start.3 = (f32[1,256,128]{2,1,0:T(8,128)S(1)}, f32[1,256,128]{2,1,0:T(8,128)S(1)}, u32[]{:S(2)}, u32[]{:S(2)}) collective-permute-start(f32[1,256,128]{2,1,0:T(8,128)S(1)} %get-tuple-element.69), channel_id=1, source_target_pairs={{0,1},{1,2},{2,3},{3,4},{4,5},{5,6},{6,7},{7,8},{8,9},{9,10},{10,1... | collective-permute-start | bytes 393224 | tf_op jit(solution)/shard_map/ppermute | solution.py:27
  95.8 1.2 copy-start.25
  131.5 5.7 %copy-start.2 = (f32[4,256,128]{2,1,0:T(8,128)}, f32[4,256,128]{2,1,0:T(8,128)S(1)}, u32[]{:S(2)}) copy-start(f32[4,256,128]{2,1,0:T(8,128)S(1)} %multiply_add_fusion.8) | copy-start | bytes 1572868
  131.5 5.7 %copy-start.5 = (f32[4,256,128]{2,1,0:T(8,128)S(1)}, f32[4,256,128]{2,1,0:T(8,128)}, u32[]{:S(2)}) copy-start(f32[4,256,128]{2,1,0:T(8,128)} %param.20) | copy-start | bytes 1572868
  131.6 5.7 %copy-start.13 = (f32[4,256,128]{2,1,0:T(8,128)S(1)}, f32[4,256,128]{2,1,0:T(8,128)}, u32[]{:S(2)}) copy-start(f32[4,256,128]{2,1,0:T(8,128)} %param.18) | copy-start | bytes 1572868
  131.6 5.7 %copy-start.15 = (f32[131072]{0:T(1024)S(1)}, f32[131072]{0:T(1024)}, u32[]{:S(2)}) copy-start(f32[131072]{0:T(1024)} %copy-done.14) | copy-start | bytes 1572868
  131.6 5.7 %copy-start.18 = (f32[4,256,128]{2,1,0:T(8,128)S(1)}, f32[4,256,128]{2,1,0:T(8,128)}, u32[]{:S(2)}) copy-start(f32[4,256,128]{2,1,0:T(8,128)} %param.25) | copy-start | bytes 1572868
  131.6 5.7 %copy-start.21 = (f32[4,256,128]{2,1,0:T(8,128)S(1)}, f32[4,256,128]{2,1,0:T(8,128)}, u32[]{:S(2)}) copy-start(f32[4,256,128]{2,1,0:T(8,128)} %param.24) | copy-start | bytes 1572868
  131.8 4.6 %collective-permute-start.4 = (f32[1,256,128]{2,1,0:T(8,128)S(1)}, f32[1,256,128]{2,1,0:T(8,128)S(1)}, u32[]{:S(2)}, u32[]{:S(2)}) collective-permute-start(f32[1,256,128]{2,1,0:T(8,128)S(1)} %get-tuple-element.58), channel_id=1, source_target_pairs={{1,0},{2,1},{3,2},{4,3},{5,4},{6,5},{7,6},{8,7},{9,8},{10,9},{11,1... | collective-permute-start | bytes 393224 | tf_op jit(solution)/shard_map/ppermute | solution.py:30
  133.2 4.0 %collective-permute-start.5 = (f32[1,256,128]{2,1,0:T(8,128)S(1)}, f32[1,256,128]{2,1,0:T(8,128)S(1)}, u32[]{:S(2)}, u32[]{:S(2)}) collective-permute-start(f32[1,256,128]{2,1,0:T(8,128)S(1)} %get-tuple-element.59), channel_id=1, source_target_pairs={{0,1},{1,2},{2,3},{3,4},{4,5},{5,6},{6,7},{7,8},{8,9},{9,10},{10,1... | collective-permute-start | bytes 393224 | tf_op jit(solution)/shard_map/ppermute | solution.py:27
  139.2 5.9 %copy-start.24 = (f32[128]{0:T(128)S(1)}, f32[128]{0:T(128)}, u32[]{:S(2)}) copy-start(f32[128]{0:T(128)} %param.27) | copy-start | bytes 1540
  139.2 5.9 %copy-start.23 = (s32[256]{0:T(256)S(1)}, s32[256]{0:T(256)}, u32[]{:S(2)}) copy-start(s32[256]{0:T(256)} %param.28) | copy-start | bytes 3076
  139.2 5.9 %copy-start.22 = (f32[256]{0:T(256)S(1)}, f32[256]{0:T(256)}, u32[]{:S(2)}) copy-start(f32[256]{0:T(256)} %param.29) | copy-start | bytes 3076
  140.4 19.2 %all-to-all-start = ((f32[4,256,128]{2,0,1:T(4,128)}), f32[4,256,128]{2,0,1:T(4,128)S(1)}, u32[]{:S(2)}, u32[]{:S(2)}) async-start(f32[4,256,128]{2,0,1:T(4,128)} %copy.117), calls=%async_computation | async-start | bytes 1048576 | tf_op jit(solution)/shard_map/all_to_all | solution.py:161
  178.5 1.3 copy-start.6
  178.5 5.7 %copy-start.7 = (f32[128,16,256]{2,0,1:T(8,128)}, f32[128,16,256]{2,0,1:T(8,128)S(1)}, u32[]{:S(2)}) copy-start(f32[128,16,256]{2,0,1:T(8,128)S(1)} %get-tuple-element.49) | copy-start | bytes 6291460
  179.8 9.5 %collective-permute-start.8 = (f32[128,1,256]{2,0,1:T(8,128)S(1)}, f32[128,1,256]{2,0,1:T(8,128)S(1)}, u32[]{:S(2)}, u32[]{:S(2)}) collective-permute-start(f32[128,1,256]{2,0,1:T(8,128)S(1)} %get-tuple-element.47), channel_id=1, source_target_pairs={{1,0},{2,1},{3,2},{4,3},{5,4},{6,5},{7,6},{8,7},{9,8},{10,9},{11,1... | collective-permute-start | bytes 393224 | tf_op jit(solution)/shard_map/ppermute | solution.py:30
  181.1 8.2 %collective-permute-start.9 = (f32[128,1,256]{2,0,1:T(8,128)S(1)}, f32[128,1,256]{2,0,1:T(8,128)S(1)}, u32[]{:S(2)}, u32[]{:S(2)}) collective-permute-start(f32[128,1,256]{2,0,1:T(8,128)S(1)} %get-tuple-element.48), channel_id=1, source_target_pairs={{0,1},{1,2},{2,3},{3,4},{4,5},{5,6},{6,7},{7,8},{8,9},{9,10},{10,1... | collective-permute-start | bytes 393224 | tf_op jit(solution)/shard_map/ppermute | solution.py:27
  184.2 5.1 %collective-permute-start.14 = (f32[128,1,256]{2,0,1:T(8,128)S(1)}, f32[128,1,256]{2,0,1:T(8,128)S(1)}, u32[]{:S(2)}, u32[]{:S(2)}) collective-permute-start(f32[128,1,256]{2,0,1:T(8,128)S(1)} %get-tuple-element.56), channel_id=1, source_target_pairs={{1,0},{2,1},{3,2},{4,3},{5,4},{6,5},{7,6},{8,7},{9,8},{10,9},{11,1... | collective-permute-start | bytes 393224 | tf_op jit(solution)/shard_map/ppermute | solution.py:30
  185.5 4.8 %collective-permute-start.15 = (f32[128,1,256]{2,0,1:T(8,128)S(1)}, f32[128,1,256]{2,0,1:T(8,128)S(1)}, u32[]{:S(2)}, u32[]{:S(2)}) collective-permute-start(f32[128,1,256]{2,0,1:T(8,128)S(1)} %get-tuple-element.57), channel_id=1, source_target_pairs={{0,1},{1,2},{2,3},{3,4},{4,5},{5,6},{6,7},{7,8},{8,9},{9,10},{10,1... | collective-permute-start | bytes 393224 | tf_op jit(solution)/shard_map/ppermute | solution.py:27
  214.5 14.8 %collective-permute-start.10 = (f32[128,1,256]{2,0,1:T(8,128)S(1)}, f32[128,1,256]{2,0,1:T(8,128)S(1)}, u32[]{:S(2)}, u32[]{:S(2)}) collective-permute-start(f32[128,1,256]{2,0,1:T(8,128)S(1)} %get-tuple-element.43), channel_id=1, source_target_pairs={{1,0},{2,1},{3,2},{4,3},{5,4},{6,5},{7,6},{8,7},{9,8},{10,9},{11,1... | collective-permute-start | bytes 393224 | tf_op jit(solution)/shard_map/ppermute | solution.py:30
  215.8 13.5 %collective-permute-start.11 = (f32[128,1,256]{2,0,1:T(8,128)S(1)}, f32[128,1,256]{2,0,1:T(8,128)S(1)}, u32[]{:S(2)}, u32[]{:S(2)}) collective-permute-start(f32[128,1,256]{2,0,1:T(8,128)S(1)} %get-tuple-element.44), channel_id=1, source_target_pairs={{0,1},{1,2},{2,3},{3,4},{4,5},{5,6},{6,7},{7,8},{8,9},{9,10},{10,1... | collective-permute-start | bytes 393224 | tf_op jit(solution)/shard_map/ppermute | solution.py:27
  222.9 6.3 %collective-permute-start.16 = (f32[128,1,256]{2,0,1:T(8,128)S(1)}, f32[128,1,256]{2,0,1:T(8,128)S(1)}, u32[]{:S(2)}, u32[]{:S(2)}) collective-permute-start(f32[128,1,256]{2,0,1:T(8,128)S(1)} %get-tuple-element.54), channel_id=1, source_target_pairs={{1,0},{2,1},{3,2},{4,3},{5,4},{6,5},{7,6},{8,7},{9,8},{10,9},{11,1... | collective-permute-start | bytes 393224 | tf_op jit(solution)/shard_map/ppermute | solution.py:30
  224.2 6.0 %collective-permute-start.17 = (f32[128,1,256]{2,0,1:T(8,128)S(1)}, f32[128,1,256]{2,0,1:T(8,128)S(1)}, u32[]{:S(2)}, u32[]{:S(2)}) collective-permute-start(f32[128,1,256]{2,0,1:T(8,128)S(1)} %get-tuple-element.55), channel_id=1, source_target_pairs={{0,1},{1,2},{2,3},{3,4},{4,5},{5,6},{6,7},{7,8},{8,9},{9,10},{10,1... | collective-permute-start | bytes 393224 | tf_op jit(solution)/shard_map/ppermute | solution.py:27
  248.9 1.3 copy-start.9
  248.9 9.3 %copy-start.10 = (f32[128,16,256]{2,0,1:T(8,128)}, f32[128,16,256]{2,0,1:T(8,128)S(1)}, u32[]{:S(2)}) copy-start(f32[128,16,256]{2,0,1:T(8,128)S(1)} %get-tuple-element.41) | copy-start | bytes 6291460
  250.2 14.5 %collective-permute-start.12 = (f32[128,1,256]{2,0,1:T(8,128)S(1)}, f32[128,1,256]{2,0,1:T(8,128)S(1)}, u32[]{:S(2)}, u32[]{:S(2)}) collective-permute-start(f32[128,1,256]{2,0,1:T(8,128)S(1)} %get-tuple-element.39), channel_id=1, source_target_pairs={{1,0},{2,1},{3,2},{4,3},{5,4},{6,5},{7,6},{8,7},{9,8},{10,9},{11,1... | collective-permute-start | bytes 393224 | tf_op jit(solution)/shard_map/ppermute | solution.py:30
  251.5 13.2 %collective-permute-start.13 = (f32[128,1,256]{2,0,1:T(8,128)S(1)}, f32[128,1,256]{2,0,1:T(8,128)S(1)}, u32[]{:S(2)}, u32[]{:S(2)}) collective-permute-start(f32[128,1,256]{2,0,1:T(8,128)S(1)} %get-tuple-element.40), channel_id=1, source_target_pairs={{0,1},{1,2},{2,3},{3,4},{4,5},{5,6},{6,7},{7,8},{8,9},{9,10},{10,1... | collective-permute-start | bytes 393224 | tf_op jit(solution)/shard_map/ppermute | solution.py:27
  258.2 6.6 %collective-permute-start.18 = (f32[128,1,256]{2,0,1:T(8,128)S(1)}, f32[128,1,256]{2,0,1:T(8,128)S(1)}, u32[]{:S(2)}, u32[]{:S(2)}) collective-permute-start(f32[128,1,256]{2,0,1:T(8,128)S(1)} %get-tuple-element.52), channel_id=1, source_target_pairs={{1,0},{2,1},{3,2},{4,3},{5,4},{6,5},{7,6},{8,7},{9,8},{10,9},{11,1... | collective-permute-start | bytes 393224 | tf_op jit(solution)/shard_map/ppermute | solution.py:30
  259.5 6.0 %collective-permute-start.19 = (f32[128,1,256]{2,0,1:T(8,128)S(1)}, f32[128,1,256]{2,0,1:T(8,128)S(1)}, u32[]{:S(2)}, u32[]{:S(2)}) collective-permute-start(f32[128,1,256]{2,0,1:T(8,128)S(1)} %get-tuple-element.53), channel_id=1, source_target_pairs={{0,1},{1,2},{2,3},{3,4},{4,5},{5,6},{6,7},{7,8},{8,9},{9,10},{10,1... | collective-permute-start | bytes 393224 | tf_op jit(solution)/shard_map/ppermute | solution.py:27
  295.9 25.4 %all-to-all-start.1 = ((f32[64,16,128]{2,1,0:T(8,128)}), f32[64,16,128]{2,1,0:T(8,128)S(1)}, u32[]{:S(2)}, u32[]{:S(2)}) async-start(f32[64,16,128]{2,1,0:T(8,128)} %fusion.57), calls=%async_computation.1 | async-start | bytes 1048576 | tf_op jit(solution)/shard_map/all_to_all | solution.py:181
  317.3 4.1 %copy-start.19 = (f32[4,256,128]{2,1,0:T(8,128)S(1)}, f32[4,256,128]{2,1,0:T(8,128)}, u32[]{:S(2)}) copy-start(f32[4,256,128]{2,1,0:T(8,128)} %param.25) | copy-start | bytes 1572868
  317.3 4.1 %copy-start.20 = (f32[4,256,128]{2,1,0:T(8,128)S(1)}, f32[4,256,128]{2,1,0:T(8,128)}, u32[]{:S(2)}) copy-start(f32[4,256,128]{2,1,0:T(8,128)} %get-tuple-element.35) | copy-start | bytes 1572868
where the time goes:
time: 324 us; the launch traced here: 323 us
  blocking collectives  95.1 us (29%)
  other arithmetic  87 us (27%)
  starting transfers between devices  73.7 us (23%)
  matrix products  23.8 us (7%)
  waiting for transfers between devices  22.8 us (7%)
  local copies, waits for them, and re-layouts  15.8 us (5%)
  between operations  5.09 us (2%)
    psum x3, blocking collectives, global_sum(): return lax.psum(values, 'sx')  95.1 us
    add x3, other arithmetic, run_wave(): following = 2.0 * current - previous + courant * model_field * stencil  49.8 us
    ppermute x10, starting transfers between devices, extended(): lax.ppermute(lax.slice_in_dim(block, block.shape[dim] - width, None, axis...  44.9 us
    add x1, other arithmetic, run_wave(): gradient = gradient + courant * stencils[number] * adjoint  21.2 us
    dot_general x1, matrix products, per_device(): jnp.dot(weight_y, depth.reshape(i_cells, planes * seis_z), precision=lax....  15.2 us
    all_to_all x1, waiting for transfers between devices, per_device(): lax.all_to_all(change, 'sx', split_axis=1, concat_axis=0, tiled=True)  14.4 us
    ppermute x10, starting transfers between devices, extended(): lax.ppermute(lax.slice_in_dim(block, 0, width, axis=dim), axis, backward)  13.2 us
    all_to_all x1, starting transfers between devices, per_device(): lax.all_to_all(restricted.reshape(i_cells, planes, depth_cells), 'sx', sp...  10.9 us
  transfers between devices with their start and end apart: 22, of which 7 were waited for; matrix products, arithmetic and copies ran while one was open for 9% of the time, Pallas kernels for 0%

commit v1 on v0

v1 whole, which is shorter than its diff:
```python
import functools

import jax
import jax.numpy as jnp
from jax import lax
from jax.experimental import pallas as pl
from jax.experimental.pallas import tpu as pltpu
from jax.sharding import PartitionSpec as P

courant = 0.25
transport = 2.0
velocity_ref = 22.5
mineral_bulk = 37.0
mineral_shear = 44.0
carbon_bulk = 0.08
brine_bulk = 2.5
mineral_density = 2.65
carbon_density = 0.7
brine_density = 1.03

F32 = jnp.float32
BF16 = jnp.bfloat16
NN = (((1,), (0,)), ((), ()))
NT = (((1,), (1,)), ((), ()))
CHUNKS = 4
ROWS = 64
PAD = 8


def split(value):
    high = value.astype(BF16)
    return high, (value - high.astype(F32)).astype(BF16)


def dot3(a_high, a_low, b_high, b_low, dims):
    def one(a, b):
        return lax.dot_general(a, b, dims, preferred_element_type=F32)

    return one(a_high, b_high) + (one(a_high, b_low) + one(a_low, b_high))


def perturb_and_slope(sat, por):
    solid = 1.0 - por
    frame = solid * solid * solid
    dry = mineral_bulk * frame
    shear = mineral_shear * frame
    biot = 1.0 - frame
    biot2 = biot * biot
    soft = sat * (1.0 / carbon_bulk) + (1.0 - sat) * (1.0 / brine_bulk)
    inv = 1.0 / (por * soft + solid * (1.0 / mineral_bulk) - dry * (1.0 / (mineral_bulk * mineral_bulk)))
    ratio = biot2 * inv
    total = dry + ratio + (4.0 / 3.0) * shear
    density = mineral_density * solid + por * (carbon_density * sat + brine_density * (1.0 - sat))
    inv_density = 1.0 / density
    change = total * inv_density * (1.0 / velocity_ref) - 1.0
    bulk_slope = -ratio * inv * por * (1.0 / carbon_bulk - 1.0 / brine_bulk)
    density_slope = por * (carbon_density - brine_density)
    slope = (bulk_slope - total * inv_density * density_slope) * inv_density * (1.0 / velocity_ref)
    return change, slope


def kernel(
    n, ni, fy, fz, sy, nx, sz,
    rs_h, st_h, tx_h, ty_h, tz_h, sl_h, po_h, bg_h, wp_h, wn_h, dr_h,
    cells, rates, yi_v, yf_v, zi_v, zf_v, yi_s, yf_s,
    pr_o, wf_o, sg_o,
    f, af, a2, src, st, tx, ty, tz, sl, po, chg, slope, pres, recv, depth, rest, ret,
    ua, ub, w5, w4, a5, a4, a3, l1, l2, mod, gz, wsend, wrecv, red,
    wzh, wzl, wyh, wyl,
    loc, hs, hr, ws, wr, rs_s, rs_r, as_s, as_r, out_s,
):
    me = lax.axis_index("sx")
    yc = sy // CHUNKS

    def wave_rows(ref):
        return ref.at[pl.ds(nx, sy * nx), :]

    def inner(ref):
        return ref.at[:, pl.ds(PAD, fy), :]

    loads = [
        pltpu.make_async_copy(a, b, loc.at[k])
        for k, (a, b) in enumerate(
            [
                (rs_h, f.at[pl.ds(1, ni), pl.ds(PAD, fy), :]),
                (st_h, st),
                (tx_h, tx),
                (ty_h, inner(ty)),
                (tz_h, tz),
                (wn_h, wave_rows(ub)),
                (sl_h, sl),
                (po_h, po),
                (bg_h, mod),
                (wp_h, wave_rows(ua)),
                (dr_h, a5),
            ]
        )
    ]
    for copy in loads:
        copy.start()

    barrier = pltpu.get_barrier_semaphore()

    def greet(o, _):
        pl.semaphore_signal(
            barrier, inc=1, device_id={"sx": lax.rem(me + o, n)},
            device_id_type=pl.DeviceIdType.MESH,
        )
        return 0

    lax.fori_loop(1, n, greet, 0)

    def remote(s, d, ssem, rsem, target):
        return pltpu.make_async_remote_copy(
            src_ref=s, dst_ref=d, send_sem=ssem, recv_sem=rsem,
            device_id={"sx": target}, device_id_type=pl.DeviceIdType.MESH,
        )

    has_left = me > 0
    has_right = me < n - 1

    def plane_copy(e, way):
        ref = (f, af)[e]
        here, there = ((1, ni + 1), (ni, 0))[way]
        return remote(
            ref.at[here, pl.ds(PAD, fy), :], ref.at[there, pl.ds(PAD, fy), :],
            hs.at[e, way], hr.at[e, way], me + (-1, 1)[way],
        )

    def wave_copy(e, q, way):
        if e == 0:
            s, d = wsend.at[e, way, q, 0], wrecv.at[e, 1 - way, q, 0]
        else:
            s, d = wsend.at[e, way, q], wrecv.at[e, 1 - way, q]
        return remote(s, d, ws.at[e, q, way], wr.at[e, q, way], me + (-1, 1)[way])

    def start_pair(make):
        pl.when(has_left)(lambda: make(0).start())
        pl.when(has_right)(lambda: make(1).start())

    def recv_pair(make):
        pl.when(has_right)(lambda: make(0).wait_recv())
        pl.when(has_left)(lambda: make(1).wait_recv())

    def sent_pair(make):
        pl.when(has_left)(lambda: make(0).wait_send())
        pl.when(has_right)(lambda: make(1).wait_send())

    rim = jnp.zeros((ni + 2, PAD, fz), F32)
    for ref in (f, af):
        ref[:, 0:PAD, :] = rim
        ref[:, PAD + fy:, :] = rim
    ty[:, 0:PAD, :] = rim[:ni]
    ty[:, PAD + fy:, :] = rim[:ni]
    zero_rows = jnp.zeros((nx, sz), F32)
    for ref in (ua, ub, w5, w4):
        ref[0:nx, :] = zero_rows
        ref[(sy + 1) * nx:, :] = zero_rows

    def zero_edge(plane, side):
        blank = jnp.zeros((fy, fz), F32)
        f[plane, pl.ds(PAD, fy), :] = blank
        af[plane, pl.ds(PAD, fy), :] = blank
        wrecv[:, side] = jnp.zeros((4, CHUNKS, 2, yc, sz), F32)

    pl.when(me == 0)(lambda: zero_edge(0, 0))
    pl.when(me == n - 1)(lambda: zero_edge(ni + 1, 1))

    cell_row = lax.shift_right_logical(cells[...], fz.bit_length() - 1)
    cell_col = cells[...] & (fz - 1)
    wells = cells.shape[1]
    rate_cols = jnp.where(
        lax.broadcasted_iota(jnp.int32, (fz, wells), 0) == cell_col, rates[...], 0.0
    )
    loads[0].wait()

    def well_plane(i):
        first = (me * ni + i) * fy
        hit = jnp.where(
            lax.broadcasted_iota(jnp.int32, (fy, wells), 0) + first == cell_row, 1.0, 0.0
        ).astype(F32)
        plane = lax.dot_general(
            hit, rate_cols, NT, precision=lax.Precision.HIGHEST, preferred_element_type=F32
        )
        src[i] = plane
        f[i + 1, pl.ds(PAD, fy), :] = f[i + 1, pl.ds(PAD, fy), :] + plane

    well_plane(0)
    well_plane(ni - 1)
    pl.semaphore_wait(barrier, n - 1)
    start_pair(functools.partial(plane_copy, 0))

    def mid_wells(i, _):
        well_plane(i)
        return 0

    lax.fori_loop(1, ni - 1, mid_wells, 0)

    row = lax.broadcasted_iota(jnp.int32, (fz, sz), 0)
    zi = zi_v[...]
    zf = zf_v[...]
    wz = jnp.where(row == zi, 1.0 - zf, 0.0) + jnp.where((row == zi + 1) & (zi >= 0), zf, 0.0)
    wzh[...], wzl[...] = split(wz)
    row = lax.broadcasted_iota(jnp.int32, (n * ni, sy), 0)
    yi = yi_v[...]
    yf = yf_v[...]
    wy = jnp.where(row == yi, 1.0 - yf, 0.0) + jnp.where((row == yi + 1) & (yi >= 0), yf, 0.0)
    wyh[...], wyl[...] = split(wy)

    for k in (1, 2, 3, 4):
        loads[k].wait()

    col = lax.broadcasted_iota(jnp.int32, (ROWS, fz), 1)

    def flow_apply(ref, i, j0):
        ext = ref[i, pl.ds(j0, ROWS + 2 * PAD), :]
        v = ext[PAD:PAD + ROWS]
        face = ty[i - 1, pl.ds(j0, ROWS + 2 * PAD), :] * (
            ext - pltpu.roll(ext, ROWS + 2 * PAD - 1, 0)
        )
        along_j = (face - pltpu.roll(face, 1, 0))[PAD:PAD + ROWS]
        up = jnp.where(col == fz - 1, 0.0, pltpu.roll(v, fz - 1, 1))
        face_z = tz[i - 1, pl.ds(j0, ROWS), :] * (v - up)
        along_k = face_z - jnp.where(col == 0, 0.0, pltpu.roll(face_z, 1, 1))
        mid = pl.ds(j0 + PAD, ROWS)
        along_i = tx[pl.ds(j0, ROWS), :] * (2.0 * v - ref[i + 1, mid, :] - ref[i - 1, mid, :])
        return v, st[i - 1, pl.ds(j0, ROWS), :] * v + along_i + along_j + along_k

    def fold(value):
        return jnp.sum(value.reshape(-1, 8, fz), axis=0)

    def image_plane(i, acc):
        def body(c, acc):
            j0 = pl.multiple_of(c * ROWS, ROWS)
            v, image = flow_apply(f, i, j0)
            af[i, pl.ds(j0 + PAD, ROWS), :] = image
            return acc[0] + fold(v * v), acc[1] + fold(v * image)

        return lax.fori_loop(0, fy // ROWS, body, acc)

    def image2_plane(i, _):
        def body(c, _):
            j0 = pl.multiple_of(c * ROWS, ROWS)
            a2[i - 1, pl.ds(j0, ROWS), :] = flow_apply(af, i, j0)[1]
            return 0

        return lax.fori_loop(0, fy // ROWS, body, 0)

    blank = jnp.zeros((8, fz), F32)
    acc = lax.fori_loop(2, ni, image_plane, (blank, blank))
    recv_pair(functools.partial(plane_copy, 0))
    acc = image_plane(1, acc)
    acc = image_plane(ni, acc)
    start_pair(functools.partial(plane_copy, 1))

    def red_copy(r, o):
        return remote(
            red.at[r, me], red.at[r, me], rs_s.at[r, o], rs_r.at[r, o], lax.rem(me + o, n)
        )

    def reduce_start(r, parts):
        rows = [jnp.sum(p, axis=0, keepdims=True) for p in parts]
        which = lax.broadcasted_iota(jnp.int32, (8, fz), 0)
        tile = jnp.zeros((8, fz), F32)
        for k, p in enumerate(rows):
            tile = jnp.where(which == k, p, tile)
        red[r, me] = tile

        def go(o, _):
            red_copy(r, o).start()
            return 0

        lax.fori_loop(1, n, go, 0)

    def reduce_end(r):
        def go(o, _):
            red_copy(r, o).wait_recv()
            return 0

        lax.fori_loop(1, n, go, 0)
        return jnp.sum(jnp.sum(red[r], axis=0), axis=1, keepdims=True)

    reduce_start(0, acc)
    lax.fori_loop(2, ni, image2_plane, 0)

    loads[5].wait()

    def first_edges(q, _):
        def body(t, _):
            for s in range(8):
                y = q * yc + t * 8 + s
                for way, x in ((0, 0), (1, nx - 1)):
                    line = ub[pl.ds(pl.multiple_of((y + 1) * nx, nx), nx), :][x:x + 1]
                    wsend[0, way, q, 0, pl.ds(t * 8 + s, 1), :] = line
            return 0

        lax.fori_loop(0, yc // 8, body, 0)
        start_pair(functools.partial(wave_copy, 0, q))
        return 0

    lax.fori_loop(0, CHUNKS, first_edges, 0)

    recv_pair(functools.partial(plane_copy, 1))
    image2_plane(1, 0)
    image2_plane(ni, 0)
    sums = reduce_end(0)
    norm0 = sums[0:1]
    curve0 = sums[1:2]
    alpha0 = norm0 / curve0

    def dots_plane(i, acc):
        def body(c, acc):
            j0 = pl.multiple_of(c * ROWS, ROWS)
            g = af[i + 1, pl.ds(j0 + PAD, ROWS), :]
            r1 = f[i + 1, pl.ds(j0 + PAD, ROWS), :] - alpha0 * g
            ar1 = g - alpha0 * a2[i, pl.ds(j0, ROWS), :]
            return acc[0] + fold(r1 * r1), acc[1] + fold(r1 * ar1), acc[2] + fold(r1 * g)

        return lax.fori_loop(0, fy // ROWS, body, acc)

    acc = lax.fori_loop(0, ni, dots_plane, (blank, blank, blank))
    reduce_start(1, acc)
    loads[6].wait()
    loads[7].wait()
    sums = reduce_end(1)
    norm1 = sums[0:1]
    beta = norm1 / norm0
    curve1 = sums[1:2] + 2.0 * beta * sums[2:3] + beta * beta * curve0
    alpha1 = norm1 / curve1
    c1 = alpha0 + alpha1 * (1.0 + beta)
    c2 = -alpha1 * alpha0

    def change_copy(o):
        d = lax.rem(me + o, n)
        return remote(
            chg.at[:, pl.ds(pl.multiple_of(d * nx, nx), nx), :],
            recv.at[pl.ds(pl.multiple_of(me * ni, ni), ni)],
            as_s.at[0, o], as_r.at[0, o], d,
        )

    def columns_of(d):
        j0 = pl.multiple_of(d * nx, nx)
        at = pl.ds(j0, nx)
        mid = pl.ds(pl.multiple_of(j0 + PAD, 8), nx)
        v = f[pl.ds(1, ni), mid, :]
        g = af[pl.ds(1, ni), mid, :]
        p = c1[0] * v + c2[0] * g
        ap = c1[0] * g + c2[0] * a2[:, at, :]
        inflow = st[:, at, :] * p - ap + src[:, at, :]
        sat = jax.nn.sigmoid(sl[:, at, :] + transport * inflow)
        value, gain = perturb_and_slope(sat, po[:, at, :])
        pres[:, at, :] = p
        slope[:, at, :] = gain
        return at, value

    def order(t):
        return 1 + lax.rem(t + n // 2 - 1, n - 1)

    def send_change(t, _):
        o = order(t)
        at, value = columns_of(lax.rem(me + o, n))
        chg[:, at, :] = value
        change_copy(o).start()
        return 0

    lax.fori_loop(0, n - 1, send_change, 0)
    _, value = columns_of(me)
    recv[pl.ds(pl.multiple_of(me * ni, ni), ni)] = value
    out_p = pltpu.make_async_copy(pres, pr_o, out_s.at[0])
    out_p.start()

    def blend_z(s):
        block = recv[pl.ds(pl.multiple_of(s * ni, ni), ni)].reshape(ni * nx, fz)
        high, low = split(block)
        depth[pl.ds(pl.multiple_of(s * ni, ni), ni)] = dot3(
            high, low, wzh[...], wzl[...], NN
        ).reshape(ni, nx, sz)

    blend_z(me)
    for k in (8, 9, 10):
        loads[k].wait()

    def take_change(t, _):
        o = order(t)
        change_copy(o).wait_recv()
        blend_z(lax.rem(me - o + n, n))
        return 0

    lax.fori_loop(0, n - 1, take_change, 0)

    zcol = lax.broadcasted_iota(jnp.int32, (nx, sz), 1)
    xrow = lax.broadcasted_iota(jnp.int32, (nx, sz), 0)

    def laplace(ref, y, low, high):
        here = pl.multiple_of((y + 1) * nx, nx)
        c = ref[pl.ds(here, nx), :]
        total = ref[pl.ds(pl.multiple_of(y * nx, nx), nx), :]
        total = total + ref[pl.ds(pl.multiple_of((y + 2) * nx, nx), nx), :]
        total = total + jnp.where(xrow == 0, low, pltpu.roll(c, 1, 0))
        total = total + jnp.where(xrow == nx - 1, high, pltpu.roll(c, nx - 1, 0))
        total = total + jnp.where(zcol == 0, 0.0, pltpu.roll(c, 1, 1))
        total = total + jnp.where(zcol == sz - 1, 0.0, pltpu.roll(c, sz - 1, 1))
        return c, total - 6.0 * c

    def stage(number):
        cur, old = ((ub, ua), (ua, ub))[(number - 1) % 2]
        e = number - 1
        w_in = (None, w5, w4, w5)[number - 1]
        w_out = (w5, w4, w5, None)[number - 1]

        def one(q, t, s, edges):
            line = t * 8 + s
            y = q * yc + line
            at = pl.ds(pl.multiple_of(y * nx, nx), nx)
            pad_at = pl.ds(pl.multiple_of((y + 1) * nx, nx), nx)
            if number == 1:
                index = yi_s[y]
                frac = yf_s[y]
                lower_w = jnp.where(index >= 0, 1.0 - frac, 0.0)
                upper_w = jnp.where(index >= 0, frac, 0.0)
                base = jnp.maximum(index, 0)
                lower = depth[base]
                upper = depth[base + 1]
                m = mod[at, :] + (lower_w * lower + upper_w * upper)
                mod[at, :] = m
            else:
                m = mod[at, :]
            c, lap = laplace(cur, y, edges[0][s:s + 1], edges[1][s:s + 1])
            new = 2.0 * c - old[pad_at, :] + courant * m * lap
            old[pad_at, :] = new
            if number == 1:
                l1[at, :] = lap
                adj = a5[at, :]
            else:
                _, lap_w = laplace(w_in, y, edges[2][s:s + 1], edges[3][s:s + 1])
                if number == 2:
                    adj = 2.0 * a5[at, :] + courant * lap_w
                    a4[at, :] = adj
                    l2[at, :] = lap
                elif number == 3:
                    late = a4[at, :]
                    adj = 2.0 * late + courant * lap_w - a5[at, :]
                    a3[at, :] = adj
                    l2[at, :] = l2[at, :] * adj + lap * late
                else:
                    adj = 2.0 * a3[at, :] + courant * lap_w - a4[at, :]
                    l1[at, :] = courant * (l1[at, :] * adj + l2[at, :] + lap * a5[at, :])
            if number < 4:
                w = m * adj
                w_out[pad_at, :] = w
                for way, x in ((0, 0), (1, nx - 1)):
                    wsend[e + 1, way, q, 0, pl.ds(line, 1), :] = new[x:x + 1]
                    wsend[e + 1, way, q, 1, pl.ds(line, 1), :] = w[x:x + 1]

        def chunk(q, _):
            recv_pair(functools.partial(wave_copy, e, q))

            def body(t, _):
                lines = pl.ds(pl.multiple_of(t * 8, 8), 8)
                edges = [
                    wrecv[e, side, q, what, lines, :]
                    for what in range(1 if number == 1 else 2)
                    for side in (0, 1)
                ]
                for s in range(8):
                    one(q, t, s, edges)
                return 0

            lax.fori_loop(0, yc // 8, body, 0)
            if number < 4:
                start_pair(functools.partial(wave_copy, e + 1, q))
            else:
                rows = pl.ds(pl.multiple_of(q * yc * nx, yc * nx), yc * nx)
                high, low = split(l1[rows, :])
                gz[rows, :] = dot3(high, low, wzh[...], wzl[...], NT)
            return 0

        lax.fori_loop(0, CHUNKS, chunk, 0)

    for number in (1, 2, 3, 4):
        stage(number)
    out_w = pltpu.make_async_copy(wave_rows(ub), wf_o, out_s.at[1])
    out_w.start()

    def restrict(x, _):
        high, low = split(gz[pl.ds(x, sy, stride=nx), :])
        rest[pl.ds(x, n * ni, stride=nx), :] = dot3(wyh[...], wyl[...], high, low, NN)
        return 0

    lax.fori_loop(0, nx, restrict, 0)

    def back_copy(o):
        d = lax.rem(me + o, n)
        return remote(
            rest.at[pl.ds(pl.multiple_of(d * ni * nx, ni * nx), ni * nx), :],
            ret.at[me], as_s.at[1, o], as_r.at[1, o], d,
        )

    def send_back(t, _):
        back_copy(order(t)).start()
        return 0

    lax.fori_loop(0, n - 1, send_back, 0)

    def finish(s, block):
        at = pl.ds(pl.multiple_of(s * nx, nx), nx)
        slope[:, at, :] = slope[:, at, :] * block.reshape(ni, nx, fz)

    finish(me, rest[pl.ds(pl.multiple_of(me * ni * nx, ni * nx), ni * nx), :])

    def take_back(t, _):
        o = order(t)
        back_copy(o).wait_recv()
        s = lax.rem(me - o + n, n)
        finish(s, ret[s])
        return 0

    lax.fori_loop(0, n - 1, take_back, 0)
    out_g = pltpu.make_async_copy(slope, sg_o, out_s.at[2])
    out_g.start()

    for e in range(2):
        sent_pair(functools.partial(plane_copy, e))

    def sent_waves(q, _):
        for e in range(4):
            sent_pair(functools.partial(wave_copy, e, q))
        return 0

    lax.fori_loop(0, CHUNKS, sent_waves, 0)

    def sent_all(o, _):
        red_copy(0, o).wait_send()
        red_copy(1, o).wait_send()
        change_copy(o).wait_send()
        back_copy(o).wait_send()
        return 0

    lax.fori_loop(1, n, sent_all, 0)
    out_p.wait()
    out_w.wait()
    out_g.wait()


def per_device(
    n, right_side, storage, trans_x, trans_y, trans_z, well_cells, well_rates, sat_logit, porosity,
    y_index, y_frac, z_index, z_frac, background, wave_prev, wave_now, data_residual,
):
    ni, fy, fz = right_side.shape
    sy, nx, sz = background.shape
    cells = ni * n
    flat = sy * nx

    def vm(*shape, dtype=F32):
        return pltpu.VMEM(shape, dtype)

    wide = (sy + 2) * nx
    scratch = [
        vm(ni + 2, fy + 2 * PAD, fz), vm(ni + 2, fy + 2 * PAD, fz), vm(ni, fy, fz), vm(ni, fy, fz),
        vm(ni, fy, fz), vm(fy, fz), vm(ni, fy + 2 * PAD, fz), vm(ni, fy, fz), vm(ni, fy, fz),
        vm(ni, fy, fz), vm(ni, fy, fz), vm(ni, fy, fz), vm(ni, fy, fz),
        vm(cells, nx, fz), vm(cells, nx, sz), vm(cells * nx, fz), vm(n, ni * nx, fz),
        vm(wide, sz), vm(wide, sz), vm(wide, sz), vm(wide, sz),
        vm(flat, sz), vm(flat, sz), vm(flat, sz), vm(flat, sz), vm(flat, sz), vm(flat, sz),
        vm(flat, fz),
        vm(4, 2, CHUNKS, 2, sy // CHUNKS, sz), vm(4, 2, CHUNKS, 2, sy // CHUNKS, sz),
        vm(2, n, 8, fz),
        vm(fz, sz, dtype=BF16), vm(fz, sz, dtype=BF16), vm(cells, sy, dtype=BF16), vm(cells, sy, dtype=BF16),
    ]
    dma = pltpu.SemaphoreType.DMA
    scratch += [
        dma((11,)), dma((2, 2)), dma((2, 2)), dma((4, CHUNKS, 2)), dma((4, CHUNKS, 2)),
        dma((2, n)), dma((2, n)), dma((2, n)), dma((2, n)), dma((3,)),
    ]
    any_spec = pl.BlockSpec(memory_space=pl.ANY)
    vmem_spec = pl.BlockSpec(memory_space=pltpu.VMEM)
    smem_spec = pl.BlockSpec(memory_space=pltpu.SMEM)
    pressure, wavefield, sat_gradient = pl.pallas_call(
        functools.partial(kernel, n, ni, fy, fz, sy, nx, sz),
        out_shape=(
            jax.ShapeDtypeStruct((ni, fy, fz), F32),
            jax.ShapeDtypeStruct((flat, sz), F32),
            jax.ShapeDtypeStruct((ni, fy, fz), F32),
        ),
        in_specs=[any_spec] * 11 + [vmem_spec] * 6 + [smem_spec] * 2,
        out_specs=(any_spec,) * 3,
        scratch_shapes=scratch,
        compiler_params=pltpu.CompilerParams(
            collective_id=0, has_side_effects=True, vmem_limit_bytes=60 * 1024 * 1024
        ),
        cost_estimate=pl.CostEstimate(flops=200000000, bytes_accessed=14000000, transcendentals=200000),
    )(
        right_side, storage, trans_x, trans_y, trans_z, sat_logit, porosity,
        background.reshape(flat, sz), wave_prev.reshape(flat, sz), wave_now.reshape(flat, sz),
        data_residual.reshape(flat, sz),
        well_cells.reshape(1, -1), well_rates.reshape(1, -1),
        y_index.reshape(1, -1), y_frac.reshape(1, -1), z_index.reshape(1, -1), z_frac.reshape(1, -1),
        y_index, y_frac,
    )
    return pressure, wavefield.reshape(sy, nx, sz), sat_gradient


def solution(mesh):
    cells = P(("grp", "sx"), None, None)
    waves = P(None, ("grp", "sx"), None)
    in_specs = (
        cells, cells, P("grp", None), cells, cells, P("grp"), P("grp"), cells, cells,
        P(), P(), P(), P(), waves, waves, waves, waves,
    )
    return jax.shard_map(
        functools.partial(per_device, mesh.shape["sx"]),
        mesh=mesh, in_specs=in_specs, out_specs=(cells, waves, cells), check_vma=False,
    )
```

time: 324 us -> 85 us (0.26)
  blocking collectives: 95.1 us -> 0 us
  other arithmetic: 87 us -> 0 us
  Pallas kernels: 0 us -> 78.3 us
  starting transfers between devices: 73.7 us -> 0 us
  matrix products: 23.8 us -> 0 us
  waiting for transfers between devices: 22.8 us -> 0 us
  local copies, waits for them, and re-layouts: 15.8 us -> 5.8 us
  between operations: 5.09 us -> 0.65 us
    psum x3 -> x0, blocking collectives: 95.1 us -> none  [global_sum(): return lax.psum(values, 'sx')]
    pallas_call x0 -> x1, Pallas kernels: none -> 78.3 us  [per_device(): pl.pallas_call(functools.partial(kernel, n, ni, fy, fz, sy, nx, sz), out_...]
    add x9 -> x0, other arithmetic: 74.4 us -> none  [the longest x3 49.8 us: run_wave(): following = 2.0 * current - previous + courant * model_field * stencil]
    ppermute x20 -> x0, starting transfers between devices: 58.1 us -> none  [the longest x10 44.9 us: extended(): lax.ppermute(lax.slice_in_dim(block, block.shape[dim] - width, None, axis...]
    dot_general x4 -> x0, matrix products: 23.8 us -> none  [the longest x1 15.2 us: per_device(): jnp.dot(weight_y, depth.reshape(i_cells, planes * seis_z), precision=lax....]
    all_to_all x2 -> x0, waiting for transfers between devices: 18.4 us -> none  [the longest x1 14.4 us: per_device(): lax.all_to_all(change, 'sx', split_axis=1, concat_axis=0, tiled=True)]
    all_to_all x2 -> x0, starting transfers between devices: 15.6 us -> none  [the longest x1 10.9 us: per_device(): lax.all_to_all(restricted.reshape(i_cells, planes, depth_cells), 'sx', sp...]
    reduce_sum x3 -> x0, other arithmetic: 6.49 us -> none  [the longest x2 3.35 us: per_device(): alpha = norm_now / global_sum(jnp.sum(direction * image))]
  transfers between devices with their start and end apart: 22 -> 0, of which waited for: 7 -> 0; matrix products, arithmetic and copies ran while one was open for 9% -> 0% of each run, Pallas kernels for 0% -> 0%
where the time goes in v1:
time: 85 us; the launch traced here: 84.7 us
  Pallas kernels  78.3 us (92%)
  local copies, waits for them, and re-layouts  5.8 us (7%)
    pallas_call x1, Pallas kernels, per_device(): pl.pallas_call(functools.partial(kernel, n, ni, fy, fz, sy, nx, sz), out_...  78.3 us
    unnamed x5, local copies, waits for them, and re-layouts  5.8 us

profile of v1, /device:TPU:0, one launch (start us, length us, event | category | flops | bytes accessed | tf_op | source)
XLA Modules:
  0.0 84.7 jit_solution(17599989321161403934)
XLA Ops:
  0.6 78.3 %shard_map.184 = (f32[4,256,128]{2,1,0:T(8,128)}, f32[2048,256]{1,0:T(8,128)}, f32[4,256,128]{2,1,0:T(8,128)}) custom-call(f32[4,256,128]{2,1,0:T(8,128)} %rs_h.1, f32[4,256,128]{2,1,0:T(8,128)} %st_h.1, f32[256,128]{1,0:T(8,128)} %tx_h.1, f32[4,256,128]{2,1,0:T(8,128)} %ty_h.1, f32[4,256,128]{2,1,0:T(8,128)} %tz_h.1, f32[4,256,128]{2,1,0:T(8,128)} %sl_h.1, ...), custom_call_target="tpu_custom_call" | custom-call | flops 200000000 | bytes 14000000 | tf_op jit(solution)/shard_map/pallas_call | solution.py:578
  78.9 1.9 %copy.23 = f32[4,256,128]{2,1,0:T(8,128)} copy(f32[4,256,128]{2,1,0:T(8,128)} %get-tuple-element.12) | data formatting | bytes 1048576
  80.8 0.0 copy-start
  80.8 3.1 %copy.24 = f32[128,16,256]{2,1,0:T(8,128)} copy(f32[128,16,256]{2,1,0:T(8,128)} %bitcast.11) | data formatting | bytes 4194304
  84.0 0.0 copy-done
  84.0 0.8 copy.25
Async XLA Ops:
  80.8 3.1 %copy-start = (f32[4,256,128]{2,1,0:T(8,128)S(1)}, f32[4,256,128]{2,1,0:T(8,128)}, u32[]{:S(2)}) copy-start(f32[4,256,128]{2,1,0:T(8,128)} %get-tuple-element.14) | copy-start | bytes 1572868

commit v2 on v1

--- a/solution.py
+++ b/solution.py
@@ -25,6 +25,7 @@
 CHUNKS = 4
 ROWS = 64
 PAD = 8
+MOVES = 4
 
 
 def split(value):
@@ -65,12 +66,13 @@
     cells, rates, yi_v, yf_v, zi_v, zf_v, yi_s, yf_s,
     pr_o, wf_o, sg_o,
     f, af, a2, src, st, tx, ty, tz, sl, po, chg, slope, pres, recv, depth, rest, ret,
-    ua, ub, w5, w4, a5, a4, a3, l1, l2, mod, gz, wsend, wrecv, red,
+    ua, ub, w5, w4, a5, a4, a3, l1, l2, mod, grad, gz, wsend, wrecv, red,
     wzh, wzl, wyh, wyl,
     loc, hs, hr, ws, wr, rs_s, rs_r, as_s, as_r, out_s,
 ):
     me = lax.axis_index("sx")
     yc = sy // CHUNKS
+    hx = nx // 2
 
     def wave_rows(ref):
         return ref.at[pl.ds(nx, sy * nx), :]
@@ -142,6 +144,12 @@
         pl.when(has_right)(lambda: make(0).wait_recv())
         pl.when(has_left)(lambda: make(1).wait_recv())
 
+    def start_way(make, way):
+        pl.when((has_left, has_right)[way])(lambda: make(way).start())
+
+    def recv_side(make, side):
+        pl.when((has_left, has_right)[side])(lambda: make(1 - side).wait_recv())
+
     def sent_pair(make):
         pl.when(has_left)(lambda: make(0).wait_send())
         pl.when(has_right)(lambda: make(1).wait_send())
@@ -320,8 +328,40 @@
 
     acc = lax.fori_loop(0, ni, dots_plane, (blank, blank, blank))
     reduce_start(1, acc)
-    loads[6].wait()
-    loads[7].wait()
+
+    zcol = lax.broadcasted_iota(jnp.int32, (nx, sz), 1)
+    xrow = lax.broadcasted_iota(jnp.int32, (nx, sz), 0)
+
+    def laplace(ref, y, low, high):
+        here = pl.multiple_of((y + 1) * nx, nx)
+        c = ref[pl.ds(here, nx), :]
+        total = ref[pl.ds(pl.multiple_of(y * nx, nx), nx), :]
+        total = total + ref[pl.ds(pl.multiple_of((y + 2) * nx, nx), nx), :]
+        total = total + jnp.where(xrow == 0, low, pltpu.roll(c, 1, 0))
+        total = total + jnp.where(xrow == nx - 1, high, pltpu.roll(c, nx - 1, 0))
+        total = total + jnp.where(zcol == 0, 0.0, pltpu.roll(c, 1, 1))
+        total = total + jnp.where(zcol == sz - 1, 0.0, pltpu.roll(c, sz - 1, 1))
+        return c, total - 6.0 * c
+
+    def first_stencil(q, _):
+        recv_pair(functools.partial(wave_copy, 0, q))
+
+        def body(t, _):
+            lines = pl.ds(pl.multiple_of(t * 8, 8), 8)
+            low = wrecv[0, 0, q, 0, lines, :]
+            high = wrecv[0, 1, q, 0, lines, :]
+            for s in range(8):
+                y = q * yc + t * 8 + s
+                _, lap = laplace(ub, y, low[s:s + 1], high[s:s + 1])
+                l1[pl.ds(pl.multiple_of(y * nx, nx), nx), :] = lap
+            return 0
+
+        lax.fori_loop(0, yc // 8, body, 0)
+        return 0
+
+    lax.fori_loop(0, CHUNKS, first_stencil, 0)
+    for k in (6, 7, 8, 9, 10):
+        loads[k].wait()
     sums = reduce_end(1)
     norm1 = sums[0:1]
     beta = norm1 / norm0
@@ -330,18 +370,18 @@
     c1 = alpha0 + alpha1 * (1.0 + beta)
     c2 = -alpha1 * alpha0
 
-    def change_copy(o):
+    def change_copy(o, h):
         d = lax.rem(me + o, n)
         return remote(
-            chg.at[:, pl.ds(pl.multiple_of(d * nx, nx), nx), :],
-            recv.at[pl.ds(pl.multiple_of(me * ni, ni), ni)],
-            as_s.at[0, o], as_r.at[0, o], d,
-        )
-
-    def columns_of(d):
-        j0 = pl.multiple_of(d * nx, nx)
-        at = pl.ds(j0, nx)
-        mid = pl.ds(pl.multiple_of(j0 + PAD, 8), nx)
+            chg.at[:, pl.ds(pl.multiple_of(d * nx + h * hx, hx), hx), :],
+            recv.at[h, pl.ds(pl.multiple_of(me * ni, ni), ni)],
+            as_s.at[h, o], as_r.at[h, o], d,
+        )
+
+    def columns_of(d, h):
+        j0 = pl.multiple_of(d * nx + h * hx, hx)
+        at = pl.ds(j0, hx)
+        mid = pl.ds(pl.multiple_of(j0 + PAD, 8), hx)
         v = f[pl.ds(1, ni), mid, :]
         g = af[pl.ds(1, ni), mid, :]
         p = c1[0] * v + c2[0] * g
@@ -356,101 +396,77 @@
     def order(t):
         return 1 + lax.rem(t + n // 2 - 1, n - 1)
 
-    def send_change(t, _):
-        o = order(t)
-        at, value = columns_of(lax.rem(me + o, n))
-        chg[:, at, :] = value
-        change_copy(o).start()
-        return 0
-
-    lax.fori_loop(0, n - 1, send_change, 0)
-    _, value = columns_of(me)
-    recv[pl.ds(pl.multiple_of(me * ni, ni), ni)] = value
+    for h in (0, 1):
+
+        def send_change(t, _):
+            o = order(t)
+            at, value = columns_of(lax.rem(me + o, n), h)
+            chg[:, at, :] = value
+            change_copy(o, h).start()
+            return 0
+
+        lax.fori_loop(0, n - 1, send_change, 0)
+    for h in (0, 1):
+        _, value = columns_of(me, h)
+        recv[h, pl.ds(pl.multiple_of(me * ni, ni), ni)] = value
     out_p = pltpu.make_async_copy(pres, pr_o, out_s.at[0])
     out_p.start()
 
-    def blend_z(s):
-        block = recv[pl.ds(pl.multiple_of(s * ni, ni), ni)].reshape(ni * nx, fz)
-        high, low = split(block)
-        depth[pl.ds(pl.multiple_of(s * ni, ni), ni)] = dot3(
-            high, low, wzh[...], wzl[...], NN
-        ).reshape(ni, nx, sz)
-
-    blend_z(me)
-    for k in (8, 9, 10):
-        loads[k].wait()
-
-    def take_change(t, _):
-        o = order(t)
-        change_copy(o).wait_recv()
-        blend_z(lax.rem(me - o + n, n))
-        return 0
-
-    lax.fori_loop(0, n - 1, take_change, 0)
-
-    zcol = lax.broadcasted_iota(jnp.int32, (nx, sz), 1)
-    xrow = lax.broadcasted_iota(jnp.int32, (nx, sz), 0)
-
-    def laplace(ref, y, low, high):
-        here = pl.multiple_of((y + 1) * nx, nx)
-        c = ref[pl.ds(here, nx), :]
-        total = ref[pl.ds(pl.multiple_of(y * nx, nx), nx), :]
-        total = total + ref[pl.ds(pl.multiple_of((y + 2) * nx, nx), nx), :]
-        total = total + jnp.where(xrow == 0, low, pltpu.roll(c, 1, 0))
-        total = total + jnp.where(xrow == nx - 1, high, pltpu.roll(c, nx - 1, 0))
-        total = total + jnp.where(zcol == 0, 0.0, pltpu.roll(c, 1, 1))
-        total = total + jnp.where(zcol == sz - 1, 0.0, pltpu.roll(c, sz - 1, 1))
-        return c, total - 6.0 * c
-
-    def stage(number):
+    group = n * ni // 2
+
+    def first_step(h):
+        def take_change(t, _):
+            change_copy(order(t), h).wait_recv()
+            return 0
+
+        lax.fori_loop(0, n - 1, take_change, 0)
+
+        def blend_z(b, _):
+            at = pl.ds(pl.multiple_of(b * group, group), group)
+            high, low = split(recv[h, at].reshape(group * hx, fz))
+            depth[h, at] = dot3(high, low, wzh[...], wzl[...], NN).reshape(group, hx, sz)
+            return 0
+
+        lax.fori_loop(0, 2, blend_z, 0)
+        x = (0, hx - 1)[h]
+
+        def chunk(q, _):
+            def body(t, _):
+                for s in range(8):
+                    line = t * 8 + s
+                    y = q * yc + line
+                    at = pl.ds(pl.multiple_of(y * nx + h * hx, hx), hx)
+                    pad_at = pl.ds(pl.multiple_of((y + 1) * nx + h * hx, hx), hx)
+                    index = yi_s[y]
+                    frac = yf_s[y]
+                    lower_w = jnp.where(index >= 0, 1.0 - frac, 0.0)
+                    upper_w = jnp.where(index >= 0, frac, 0.0)
+                    base = jnp.maximum(index, 0)
+                    lower = depth[h, base]
+                    upper = depth[h, base + 1]
+                    m = mod[at, :] + (lower_w * lower + upper_w * upper)
+                    mod[at, :] = m
+                    new = 2.0 * ub[pad_at, :] - ua[pad_at, :] + courant * m * l1[at, :]
+                    w = m * a5[at, :]
+                    ua[pad_at, :] = new
+                    w5[pad_at, :] = w
+                    wsend[1, h, q, 0, pl.ds(line, 1), :] = new[x:x + 1]
+                    wsend[1, h, q, 1, pl.ds(line, 1), :] = w[x:x + 1]
+                return 0
+
+            lax.fori_loop(0, yc // 8, body, 0)
+            start_way(functools.partial(wave_copy, 1, q), h)
+            return 0
+
+        lax.fori_loop(0, CHUNKS, chunk, 0)
+
+    first_step(0)
+    first_step(1)
+
+    def middle_step(number):
         cur, old = ((ub, ua), (ua, ub))[(number - 1) % 2]
+        w_in, w_out = ((w5, w4), (w4, w5))[number - 2]
         e = number - 1
-        w_in = (None, w5, w4, w5)[number - 1]
-        w_out = (w5, w4, w5, None)[number - 1]
-
-        def one(q, t, s, edges):
-            line = t * 8 + s
-            y = q * yc + line
-            at = pl.ds(pl.multiple_of(y * nx, nx), nx)
-            pad_at = pl.ds(pl.multiple_of((y + 1) * nx, nx), nx)
-            if number == 1:
-                index = yi_s[y]
-                frac = yf_s[y]
-                lower_w = jnp.where(index >= 0, 1.0 - frac, 0.0)
-                upper_w = jnp.where(index >= 0, frac, 0.0)
-                base = jnp.maximum(index, 0)
-                lower = depth[base]
-                upper = depth[base + 1]
-                m = mod[at, :] + (lower_w * lower + upper_w * upper)
-                mod[at, :] = m
-            else:
-                m = mod[at, :]
-            c, lap = laplace(cur, y, edges[0][s:s + 1], edges[1][s:s + 1])
-            new = 2.0 * c - old[pad_at, :] + courant * m * lap
-            old[pad_at, :] = new
-            if number == 1:
-                l1[at, :] = lap
-                adj = a5[at, :]
-            else:
-                _, lap_w = laplace(w_in, y, edges[2][s:s + 1], edges[3][s:s + 1])
-                if number == 2:
-                    adj = 2.0 * a5[at, :] + courant * lap_w
-                    a4[at, :] = adj
-                    l2[at, :] = lap
-                elif number == 3:
-                    late = a4[at, :]
-                    adj = 2.0 * late + courant * lap_w - a5[at, :]
-                    a3[at, :] = adj
-                    l2[at, :] = l2[at, :] * adj + lap * late
-                else:
-                    adj = 2.0 * a3[at, :] + courant * lap_w - a4[at, :]
-                    l1[at, :] = courant * (l1[at, :] * adj + l2[at, :] + lap * a5[at, :])
-            if number < 4:
-                w = m * adj
-                w_out[pad_at, :] = w
-                for way, x in ((0, 0), (1, nx - 1)):
-                    wsend[e + 1, way, q, 0, pl.ds(line, 1), :] = new[x:x + 1]
-                    wsend[e + 1, way, q, 1, pl.ds(line, 1), :] = w[x:x + 1]
 
         def chunk(q, _):
             recv_pair(functools.partial(wave_copy, e, q))
@@ -458,64 +474,136 @@
             def body(t, _):
                 lines = pl.ds(pl.multiple_of(t * 8, 8), 8)
                 edges = [
-                    wrecv[e, side, q, what, lines, :]
-                    for what in range(1 if number == 1 else 2)
-                    for side in (0, 1)
+                    wrecv[e, side, q, what, lines, :] for what in range(2) for side in (0, 1)
                 ]
                 for s in range(8):
-                    one(q, t, s, edges)
+                    line = t * 8 + s
+                    y = q * yc + line
+                    at = pl.ds(pl.multiple_of(y * nx, nx), nx)
+                    pad_at = pl.ds(pl.multiple_of((y + 1) * nx, nx), nx)
+                    m = mod[at, :]
+                    c, lap = laplace(cur, y, edges[0][s:s + 1], edges[1][s:s + 1])
+                    new = 2.0 * c - old[pad_at, :] + courant * m * lap
+                    _, lap_w = laplace(w_in, y, edges[2][s:s + 1], edges[3][s:s + 1])
+                    if number == 2:
+                        adj = 2.0 * a5[at, :] + courant * lap_w
+                        a4[at, :] = adj
+                        l2[at, :] = lap
+                    else:
+                        late = a4[at, :]
+                        adj = 2.0 * late + courant * lap_w - a5[at, :]
+                        a3[at, :] = adj
+                        l2[at, :] = l2[at, :] * adj + lap * late
+                    w = m * adj
+                    old[pad_at, :] = new
+                    w_out[pad_at, :] = w
+                    for way, x in ((0, 0), (1, nx - 1)):
+                        wsend[e + 1, way, q, 0, pl.ds(line, 1), :] = new[x:x + 1]
+                        wsend[e + 1, way, q, 1, pl.ds(line, 1), :] = w[x:x + 1]
                 return 0
 
             lax.fori_loop(0, yc // 8, body, 0)
-            if number < 4:
-                start_pair(functools.partial(wave_copy, e + 1, q))
-            else:
-                rows = pl.ds(pl.multiple_of(q * yc * nx, yc * nx), yc * nx)
-                high, low = split(l1[rows, :])
-                gz[rows, :] = dot3(high, low, wzh[...], wzl[...], NT)
+            start_pair(functools.partial(wave_copy, e + 1, q))
             return 0
 
         lax.fori_loop(0, CHUNKS, chunk, 0)
 
-    for number in (1, 2, 3, 4):
-        stage(number)
+    middle_step(2)
+    middle_step(3)
+
+    hcol = lax.broadcasted_iota(jnp.int32, (hx, sz), 1)
+    hrow = lax.broadcasted_iota(jnp.int32, (hx, sz), 0)
+
+    def half_laplace(ref, y, h, edge):
+        def part(row, g):
+            return ref[pl.ds(pl.multiple_of(row * nx + g * hx, hx), hx), :]
+
+        c = part(y + 1, h)
+        other = part(y + 1, 1 - h)
+        low, high = ((edge, other[0:1]), (other[hx - 1:hx], edge))[h]
+        total = part(y, h) + part(y + 2, h)
+        total = total + jnp.where(hrow == 0, low, pltpu.roll(c, 1, 0))
+        total = total + jnp.where(hrow == hx - 1, high, pltpu.roll(c, hx - 1, 0))
+        total = total + jnp.where(hcol == 0, 0.0, pltpu.roll(c, 1, 1))
+        total = total + jnp.where(hcol == sz - 1, 0.0, pltpu.roll(c, sz - 1, 1))
+        return total - 6.0 * c
+
+    def back_copy(o, h):
+        d = lax.rem(me + o, n)
+        size = ni * hx
+        return remote(
+            rest.at[h, pl.ds(pl.multiple_of(d * size, size), size), :],
+            ret.at[h, me], as_s.at[2 + h, o], as_r.at[2 + h, o], d,
+        )
+
+    def last_step(h):
+        def chunk(q, _):
+            recv_side(functools.partial(wave_copy, 3, q), h)
+
+            def body(t, _):
+                lines = pl.ds(pl.multiple_of(t * 8, 8), 8)
+                edge_u = wrecv[3, h, q, 0, lines, :]
+                edge_w = wrecv[3, h, q, 1, lines, :]
+                for s in range(8):
+                    y = q * yc + t * 8 + s
+                    at = pl.ds(pl.multiple_of(y * nx + h * hx, hx), hx)
+                    lap = half_laplace(ua, y, h, edge_u[s:s + 1])
+                    lap_w = half_laplace(w5, y, h, edge_w[s:s + 1])
+                    adj = 2.0 * a3[at, :] + courant * lap_w - a4[at, :]
+                    grad[h, pl.ds(pl.multiple_of(y * hx, hx), hx), :] = courant * (
+                        l1[at, :] * adj + l2[at, :] + lap * a5[at, :]
+                    )
+                    l2[at, :] = lap
+                return 0
+
+            lax.fori_loop(0, yc // 8, body, 0)
+            rows = pl.ds(pl.multiple_of(q * yc * hx, yc * hx), yc * hx)
+            high, low = split(grad[h, rows, :])
+            gz[h, rows, :] = dot3(high, low, wzh[...], wzl[...], NT)
+            return 0
+
+        lax.fori_loop(0, CHUNKS, chunk, 0)
+
+        for x in range(hx):
+            high, low = split(gz[h, pl.ds(x, sy, stride=hx), :])
+            rest[h, pl.ds(x, n * ni, stride=hx), :] = dot3(wyh[...], wyl[...], high, low, NN)
+
+        def send_back(t, _):
+            back_copy(order(t), h).start()
+            return 0
+
+        lax.fori_loop(0, n - 1, send_back, 0)
+
+    last_step(0)
+    last_step(1)
+
+    def last_wave(t, _):
+        rows = 8 * nx
+        at = pl.ds(pl.multiple_of(t * rows, rows), rows)
+        pad_at = pl.ds(pl.multiple_of(t * rows + nx, nx), rows)
+        ub[pad_at, :] = 2.0 * ua[pad_at, :] - ub[pad_at, :] + courant * mod[at, :] * l2[at, :]
+        return 0
+
+    lax.fori_loop(0, sy // 8, last_wave, 0)
     out_w = pltpu.make_async_copy(wave_rows(ub), wf_o, out_s.at[1])
     out_w.start()
 
-    def restrict(x, _):
-        high, low = split(gz[pl.ds(x, sy, stride=nx), :])
-        rest[pl.ds(x, n * ni, stride=nx), :] = dot3(wyh[...], wyl[...], high, low, NN)
-        return 0
-
-    lax.fori_loop(0, nx, restrict, 0)
-
-    def back_copy(o):
-        d = lax.rem(me + o, n)
-        return remote(
-            rest.at[pl.ds(pl.multiple_of(d * ni * nx, ni * nx), ni * nx), :],
-            ret.at[me], as_s.at[1, o], as_r.at[1, o], d,
-        )
-
-    def send_back(t, _):
-        back_copy(order(t)).start()
-        return 0
-
-    lax.fori_loop(0, n - 1, send_back, 0)
-
-    def finish(s, block):
-        at = pl.ds(pl.multiple_of(s * nx, nx), nx)
-        slope[:, at, :] = slope[:, at, :] * block.reshape(ni, nx, fz)
-
-    finish(me, rest[pl.ds(pl.multiple_of(me * ni * nx, ni * nx), ni * nx), :])
-
-    def take_back(t, _):
-        o = order(t)
-        back_copy(o).wait_recv()
-        s = lax.rem(me - o + n, n)
-        finish(s, ret[s])
-        return 0
-
-    lax.fori_loop(0, n - 1, take_back, 0)
+    def finish(s, h, block):
+        at = pl.ds(pl.multiple_of(s * nx + h * hx, hx), hx)
+        slope[:, at, :] = slope[:, at, :] * block.reshape(ni, hx, fz)
+
+    for h in (0, 1):
+        size = ni * hx
+        finish(me, h, rest[h, pl.ds(pl.multiple_of(me * size, size), size), :])
+
+        def take_back(t, _):
+            o = order(t)
+            back_copy(o, h).wait_recv()
+            s = lax.rem(me - o + n, n)
+            finish(s, h, ret[h, s])
+            return 0
+
+        lax.fori_loop(0, n - 1, take_back, 0)
     out_g = pltpu.make_async_copy(slope, sg_o, out_s.at[2])
     out_g.start()
 
@@ -532,14 +620,37 @@
     def sent_all(o, _):
         red_copy(0, o).wait_send()
         red_copy(1, o).wait_send()
-        change_copy(o).wait_send()
-        back_copy(o).wait_send()
+        for h in (0, 1):
+            change_copy(o, h).wait_send()
+            back_copy(o, h).wait_send()
         return 0
 
     lax.fori_loop(1, n, sent_all, 0)
     out_p.wait()
     out_w.wait()
     out_g.wait()
+
+
+def move_out(*refs):
+    ins, outs, held, arrive, leave = refs[:3], refs[3:6], refs[6:9], refs[9], refs[10]
+    moves = []
+    for k in range(3):
+        for part in range(MOVES):
+            rows = ins[k].shape[0] // MOVES
+            at = pl.ds(part * rows, rows)
+            moves.append(
+                (
+                    pltpu.make_async_copy(ins[k].at[at], held[k].at[at], arrive.at[k, part]),
+                    pltpu.make_async_copy(held[k].at[at], outs[k].at[at], leave.at[k, part]),
+                )
+            )
+    for come, _ in moves:
+        come.start()
+    for come, go in moves:
+        come.wait()
+        go.start()
+    for _, go in moves:
+        go.wait()
 
 
 def per_device(
@@ -559,10 +670,11 @@
         vm(ni + 2, fy + 2 * PAD, fz), vm(ni + 2, fy + 2 * PAD, fz), vm(ni, fy, fz), vm(ni, fy, fz),
         vm(ni, fy, fz), vm(fy, fz), vm(ni, fy + 2 * PAD, fz), vm(ni, fy, fz), vm(ni, fy, fz),
         vm(ni, fy, fz), vm(ni, fy, fz), vm(ni, fy, fz), vm(ni, fy, fz),
-        vm(cells, nx, fz), vm(cells, nx, sz), vm(cells * nx, fz), vm(n, ni * nx, fz),
+        vm(2, cells, nx // 2, fz), vm(2, cells, nx // 2, sz), vm(2, cells * nx // 2, fz),
+        vm(2, n, ni * nx // 2, fz),
         vm(wide, sz), vm(wide, sz), vm(wide, sz), vm(wide, sz),
         vm(flat, sz), vm(flat, sz), vm(flat, sz), vm(flat, sz), vm(flat, sz), vm(flat, sz),
-        vm(flat, fz),
+        vm(2, flat // 2, sz), vm(2, flat // 2, fz),
         vm(4, 2, CHUNKS, 2, sy // CHUNKS, sz), vm(4, 2, CHUNKS, 2, sy // CHUNKS, sz),
         vm(2, n, 8, fz),
         vm(fz, sz, dtype=BF16), vm(fz, sz, dtype=BF16), vm(cells, sy, dtype=BF16), vm(cells, sy, dtype=BF16),
@@ -570,7 +682,7 @@
     dma = pltpu.SemaphoreType.DMA
     scratch += [
         dma((11,)), dma((2, 2)), dma((2, 2)), dma((4, CHUNKS, 2)), dma((4, CHUNKS, 2)),
-        dma((2, n)), dma((2, n)), dma((2, n)), dma((2, n)), dma((3,)),
+        dma((2, n)), dma((2, n)), dma((4, n)), dma((4, n)), dma((3,)),
     ]
     any_spec = pl.BlockSpec(memory_space=pl.ANY)
     vmem_spec = pl.BlockSpec(memory_space=pltpu.VMEM)
@@ -597,6 +709,15 @@
         y_index.reshape(1, -1), y_frac.reshape(1, -1), z_index.reshape(1, -1), z_frac.reshape(1, -1),
         y_index, y_frac,
     )
+    results = (pressure, wavefield, sat_gradient)
+    pressure, wavefield, sat_gradient = pl.pallas_call(
+        move_out,
+        out_shape=tuple(jax.ShapeDtypeStruct(r.shape, F32) for r in results),
+        in_specs=[any_spec] * 3,
+        out_specs=(any_spec,) * 3,
+        scratch_shapes=[vm(*r.shape) for r in results] + [dma((3, MOVES)), dma((3, MOVES))],
+        compiler_params=pltpu.CompilerParams(vmem_limit_bytes=32 * 1024 * 1024),
+    )(*results)
     return pressure, wavefield.reshape(sy, nx, sz), sat_gradient
 
 

time: 85 us -> 79.4 us (0.934)
  Pallas kernels: 78.3 us -> 74.8 us
  local copies, waits for them, and re-layouts: 5.8 us -> 3.67 us
    pallas_call x1, Pallas kernels: 78.3 us -> 71.5 us  [per_device(): pl.pallas_call(functools.partial(kernel, n, ni, fy, fz, sy, nx, sz), out_...]
    pallas_call x0 -> x1, Pallas kernels: none -> 3.31 us  [per_device(): pl.pallas_call(move_out, out_shape=tuple((jax.ShapeDtypeStruct(r.shape, F...]
    unnamed x5 -> x6, local copies, waits for them, and re-layouts: 5.8 us -> 3.67 us
where the time goes in v2:
time: 79.4 us; the launch traced here: 79.2 us
  Pallas kernels  74.8 us (94%)
  local copies, waits for them, and re-layouts  3.67 us (5%)
    pallas_call x1, Pallas kernels, per_device(): pl.pallas_call(functools.partial(kernel, n, ni, fy, fz, sy, nx, sz), out_...  71.5 us
    unnamed x6, local copies, waits for them, and re-layouts  3.67 us
    pallas_call x1, Pallas kernels, per_device(): pl.pallas_call(move_out, out_shape=tuple((jax.ShapeDtypeStruct(r.shape, F...  3.31 us

profile of v2, /device:TPU:0, one launch (start us, length us, event | category | flops | bytes accessed | tf_op | source)
XLA Modules:
  0.0 79.2 jit_solution(13932215598216011112)
XLA Ops:
  0.6 71.5 %shard_map.184 = (f32[4,256,128]{2,1,0:T(8,128)}, f32[2048,256]{1,0:T(8,128)}, f32[4,256,128]{2,1,0:T(8,128)}) custom-call(f32[4,256,128]{2,1,0:T(8,128)} %rs_h.1, f32[4,256,128]{2,1,0:T(8,128)} %st_h.1, f32[256,128]{1,0:T(8,128)} %tx_h.1, f32[4,256,128]{2,1,0:T(8,128)} %ty_h.1, f32[4,256,128]{2,1,0:T(8,128)} %tz_h.1, f32[4,256,128]{2,1,0:T(8,128)} %sl_h.1, ...), custom_call_target="tpu_custom_call" | custom-call | flops 200000000 | bytes 14000000 | tf_op jit(solution)/shard_map/pallas_call | solution.py:690
  72.2 0.0 copy-start
  72.2 1.6 %copy-done = f32[2048,256]{1,0:T(8,128)S(1)} copy-done((f32[2048,256]{1,0:T(8,128)S(1)}, f32[2048,256]{1,0:T(8,128)}, u32[]{:S(2)}) %copy-start) | copy-done | bytes 2097176
  73.8 0.0 copy-start.1
  73.8 1.0 %copy-done.1 = f32[4,256,128]{2,1,0:T(8,128)S(1)} copy-done((f32[4,256,128]{2,1,0:T(8,128)S(1)}, f32[4,256,128]{2,1,0:T(8,128)}, u32[]{:S(2)}) %copy-start.1) | copy-done | bytes 524312
  74.8 0.0 copy-start.2
  74.8 1.0 %copy-done.2 = f32[4,256,128]{2,1,0:T(8,128)S(1)} copy-done((f32[4,256,128]{2,1,0:T(8,128)S(1)}, f32[4,256,128]{2,1,0:T(8,128)}, u32[]{:S(2)}) %copy-start.2) | copy-done | bytes 524312
  75.8 3.3 %shard_map.185 = (f32[4,256,128]{2,1,0:T(8,128)}, f32[2048,256]{1,0:T(8,128)}, f32[4,256,128]{2,1,0:T(8,128)}) custom-call(f32[4,256,128]{2,1,0:T(8,128)S(1)} %copy-done.1, f32[2048,256]{1,0:T(8,128)S(1)} %copy-done, f32[4,256,128]{2,1,0:T(8,128)S(1)} %copy-done.2), custom_call_target="tpu_custom_call" | custom-call | tf_op jit(solution)/shard_map/pallas_call | solution.py:713
Async XLA Ops:
  72.2 1.6 %copy-start = (f32[2048,256]{1,0:T(8,128)S(1)}, f32[2048,256]{1,0:T(8,128)}, u32[]{:S(2)}) copy-start(f32[2048,256]{1,0:T(8,128)} %get-tuple-element.10.refs_1_) | copy-start | bytes 6291460
  73.8 1.0 %copy-start.1 = (f32[4,256,128]{2,1,0:T(8,128)S(1)}, f32[4,256,128]{2,1,0:T(8,128)}, u32[]{:S(2)}) copy-start(f32[4,256,128]{2,1,0:T(8,128)} %get-tuple-element.9.refs_0_) | copy-start | bytes 1572868
  74.8 1.0 %copy-start.2 = (f32[4,256,128]{2,1,0:T(8,128)S(1)}, f32[4,256,128]{2,1,0:T(8,128)}, u32[]{:S(2)}) copy-start(f32[4,256,128]{2,1,0:T(8,128)} %get-tuple-element.11.refs_2_) | copy-start | bytes 1572868

commit v3 on v2

--- a/solution.py
+++ b/solution.py
@@ -256,10 +256,11 @@
 
     blank = jnp.zeros((8, fz), F32)
     acc = lax.fori_loop(2, ni, image_plane, (blank, blank))
-    recv_pair(functools.partial(plane_copy, 0))
+    recv_side(functools.partial(plane_copy, 0), 0)
     acc = image_plane(1, acc)
+    start_way(functools.partial(plane_copy, 1), 0)
+    recv_side(functools.partial(plane_copy, 0), 1)
     acc = image_plane(ni, acc)
-    start_pair(functools.partial(plane_copy, 1))
 
     def red_copy(r, o):
         return remote(
@@ -289,6 +290,7 @@
         return jnp.sum(jnp.sum(red[r], axis=0), axis=1, keepdims=True)
 
     reduce_start(0, acc)
+    start_way(functools.partial(plane_copy, 1), 1)
     lax.fori_loop(2, ni, image2_plane, 0)
 
     loads[5].wait()
@@ -308,9 +310,6 @@
 
     lax.fori_loop(0, CHUNKS, first_edges, 0)
 
-    recv_pair(functools.partial(plane_copy, 1))
-    image2_plane(1, 0)
-    image2_plane(ni, 0)
     sums = reduce_end(0)
     norm0 = sums[0:1]
     curve0 = sums[1:2]
@@ -326,7 +325,13 @@
 
         return lax.fori_loop(0, fy // ROWS, body, acc)
 
-    acc = lax.fori_loop(0, ni, dots_plane, (blank, blank, blank))
+    acc = lax.fori_loop(1, ni - 1, dots_plane, (blank, blank, blank))
+    recv_side(functools.partial(plane_copy, 1), 0)
+    image2_plane(1, 0)
+    acc = dots_plane(0, acc)
+    recv_side(functools.partial(plane_copy, 1), 1)
+    image2_plane(ni, 0)
+    acc = dots_plane(ni - 1, acc)
     reduce_start(1, acc)
 
     zcol = lax.broadcasted_iota(jnp.int32, (nx, sz), 1)
@@ -716,7 +721,7 @@
         in_specs=[any_spec] * 3,
         out_specs=(any_spec,) * 3,
         scratch_shapes=[vm(*r.shape) for r in results] + [dma((3, MOVES)), dma((3, MOVES))],
-        compiler_params=pltpu.CompilerParams(vmem_limit_bytes=32 * 1024 * 1024),
+        compiler_params=pltpu.CompilerParams(vmem_limit_bytes=60 * 1024 * 1024),
     )(*results)
     return pressure, wavefield.reshape(sy, nx, sz), sat_gradient
 

time: 79.4 us -> 75.5 us (0.951)
  local copies, waits for them, and re-layouts: 3.67 us -> 0 us
    unnamed x6 -> x0, local copies, waits for them, and re-layouts: 3.67 us -> none
where the time goes in v3:
time: 75.5 us; the launch traced here: 75.3 us
  Pallas kernels  74.7 us (99%)
    pallas_call x1, Pallas kernels, per_device(): pl.pallas_call(functools.partial(kernel, n, ni, fy, fz, sy, nx, sz), out_...  71.7 us
    pallas_call x1, Pallas kernels, per_device(): pl.pallas_call(move_out, out_shape=tuple((jax.ShapeDtypeStruct(r.shape, F...  2.99 us

profile of v3, /device:TPU:0, one launch (start us, length us, event | category | flops | bytes accessed | tf_op | source)
XLA Modules:
  0.0 75.3 jit_solution(17059688128403289801)
XLA Ops:
  0.6 71.7 %shard_map.184 = (f32[4,256,128]{2,1,0:T(8,128)}, f32[2048,256]{1,0:T(8,128)}, f32[4,256,128]{2,1,0:T(8,128)}) custom-call(f32[4,256,128]{2,1,0:T(8,128)} %rs_h.1, f32[4,256,128]{2,1,0:T(8,128)} %st_h.1, f32[256,128]{1,0:T(8,128)} %tx_h.1, f32[4,256,128]{2,1,0:T(8,128)} %ty_h.1, f32[4,256,128]{2,1,0:T(8,128)} %tz_h.1, f32[4,256,128]{2,1,0:T(8,128)} %sl_h.1, ...), custom_call_target="tpu_custom_call" | custom-call | flops 200000000 | bytes 14000000 | tf_op jit(solution)/shard_map/pallas_call | solution.py:695
  72.4 3.0 %shard_map.185 = (f32[4,256,128]{2,1,0:T(8,128)}, f32[2048,256]{1,0:T(8,128)}, f32[4,256,128]{2,1,0:T(8,128)}) custom-call(f32[4,256,128]{2,1,0:T(8,128)} %get-tuple-element.9.refs_0_, f32[2048,256]{1,0:T(8,128)} %get-tuple-element.10.refs_1_, f32[4,256,128]{2,1,0:T(8,128)} %get-tuple-element.11.refs_2_), custom_call_target="tpu_custom_call" | custom-call | tf_op jit(solution)/shard_map/pallas_call | solution.py:718

commit v4 on v3

--- a/solution.py
+++ b/solution.py
@@ -399,7 +399,8 @@
         return at, value
 
     def order(t):
-        return 1 + lax.rem(t + n // 2 - 1, n - 1)
+        step = (t + 1) // 2
+        return n // 2 + step * (1 - 2 * lax.rem(t + 1, 2))
 
     for h in (0, 1):
 

time: 75.5 us -> 73.5 us (0.974)
  Pallas kernels: 74.7 us -> 72.7 us
    pallas_call x1, Pallas kernels: 71.7 us -> 69.7 us  [per_device(): pl.pallas_call(functools.partial(kernel, n, ni, fy, fz, sy, nx, sz), out_...]
where the time goes in v4:
time: 73.5 us; the launch traced here: 73.3 us
  Pallas kernels  72.7 us (99%)
    pallas_call x1, Pallas kernels, per_device(): pl.pallas_call(functools.partial(kernel, n, ni, fy, fz, sy, nx, sz), out_...  69.7 us
    pallas_call x1, Pallas kernels, per_device(): pl.pallas_call(move_out, out_shape=tuple((jax.ShapeDtypeStruct(r.shape, F...  2.99 us

profile of v4, /device:TPU:0, one launch (start us, length us, event | category | flops | bytes accessed | tf_op | source)
XLA Modules:
  0.0 73.3 jit_solution(16050838469218885725)
XLA Ops:
  0.6 69.7 %shard_map.184 = (f32[4,256,128]{2,1,0:T(8,128)}, f32[2048,256]{1,0:T(8,128)}, f32[4,256,128]{2,1,0:T(8,128)}) custom-call(f32[4,256,128]{2,1,0:T(8,128)} %rs_h.1, f32[4,256,128]{2,1,0:T(8,128)} %st_h.1, f32[256,128]{1,0:T(8,128)} %tx_h.1, f32[4,256,128]{2,1,0:T(8,128)} %ty_h.1, f32[4,256,128]{2,1,0:T(8,128)} %tz_h.1, f32[4,256,128]{2,1,0:T(8,128)} %sl_h.1, ...), custom_call_target="tpu_custom_call" | custom-call | flops 200000000 | bytes 14000000 | tf_op jit(solution)/shard_map/pallas_call | solution.py:696
  70.3 3.0 %shard_map.185 = (f32[4,256,128]{2,1,0:T(8,128)}, f32[2048,256]{1,0:T(8,128)}, f32[4,256,128]{2,1,0:T(8,128)}) custom-call(f32[4,256,128]{2,1,0:T(8,128)} %get-tuple-element.9.refs_0_, f32[2048,256]{1,0:T(8,128)} %get-tuple-element.10.refs_1_, f32[4,256,128]{2,1,0:T(8,128)} %get-tuple-element.11.refs_2_), custom_call_target="tpu_custom_call" | custom-call | tf_op jit(solution)/shard_map/pallas_call | solution.py:719
